TPU v7x, 32 devices: a whole 2x2x4 slice. The times are simulated.
32 devices in a mesh: bead: 8 (over z, x), space: 4 (over y, core).
Axes of the slice: x: 2, y: 2, z: 4, core: 2. Of those that a mesh axis runs over, the one named last changes fastest.
Arguments:
- positions: float32 [32, 64, 3, 128], P('bead', 'space'), may hold values from 0 to 1
- momenta: float32 [32, 64, 3, 128], P('bead', 'space'), may hold values from -3 to 3
- noise: float32 [32, 64, 3, 128], P('bead', 'space'), may hold values from -6 to 6
- atom_types: int32 [64, 128], P('space'), may hold values from 0 to 3
- occupancy: int32 [64], P('space'), may hold values from 64 to 128, as said below
- type_sigma: float32 [4], replicated, may hold values from 0.2 to 0.4
- type_eps: float32 [4], replicated, may hold values from 0.5 to 2
- type_mass: float32 [4], replicated, may hold values from 1 to 4
Outputs:
- new_positions: float32 [32, 64, 3, 128], P('bead', 'space')
- new_momenta: float32 [32, 64, 3, 128], P('bead', 'space')
Inputs may be any that keep to these rules, and one draw needn't show every extreme that they name: `occupancy`: in each domain of 16 consecutive cells some cell holds 128 atoms.
All inputs are finite; a program needn't handle non-finite values.
Results may differ from a plain program's by a relative error of at most 0.0002.
Values sent between devices are 32-bit elements; how exact they have to be, the bound alone decides.
No kernel may reach another device: no remote copies, remote signals or barrier semaphores. Data moves between devices by JAX's collectives and lax.ppermute only.
A program may use at most 64 MiB of HBM per device.

v0:
```python
import jax
import jax.numpy as jnp
from jax import lax
from jax.sharding import PartitionSpec as P

PC = 8
GY = 4
GZ = 4


TIME_STEP = 0.05
INVERSE_TEMP = 32.0
CENTROID_FRICTION = 1.0
INNER_CUT = 0.5
OUTER_CUT = 1.0
precise = lax.Precision.HIGHEST


def with_halo(cells, sides, width):
    for axis, dim in sides:
        count = lax.axis_size(axis)
        head = lax.slice_in_dim(cells, 0, width, axis=dim)
        tail = lax.slice_in_dim(cells, cells.shape[dim] - width, cells.shape[dim], axis=dim)
        cells = jnp.concatenate(
            [
                lax.ppermute(tail, axis, [(i, (i + 1) % count) for i in range(count)]),
                cells,
                lax.ppermute(head, axis, [((i + 1) % count, i) for i in range(count)]),
            ],
            axis=dim,
        )
    return cells


def stencil_table(cell_total, per_domain, depth_z, height_y):
    in_domain = jnp.arange(cell_total) % per_domain
    across = in_domain // depth_z
    upward = in_domain % depth_z
    offsets = jnp.arange(27)
    step_x = offsets // 9 - 1
    step_y = offsets // 3 % 3 - 1
    step_z = offsets % 3 - 1
    target_y = across[:, None] + step_y[None, :]
    target_z = upward[:, None] + step_z[None, :]
    inside = (target_y >= 0) & (target_y < height_y) & (target_z >= 0) & (target_z < depth_z)
    entry = (step_x[None, :] + 1) * per_domain + target_y * depth_z + target_z
    return jnp.where(inside, entry, 3 * per_domain)


def mode_table(number):
    bead_rows = jnp.arange(number, dtype=jnp.float32)[:, None]
    column = jnp.arange(number, dtype=jnp.float32)[None, :]
    phases = 2.0 * jnp.pi * bead_rows * column / number
    factor = jnp.sqrt(2.0 / number)
    middle = jnp.cos(jnp.pi * bead_rows) / jnp.sqrt(float(number))
    matrix = jnp.where(column < number / 2, factor * jnp.cos(phases), factor * jnp.sin(phases))
    matrix = jnp.where(column == number / 2, middle, matrix)
    matrix = jnp.where(column == 0, 1.0 / jnp.sqrt(float(number)), matrix)
    return matrix


def contract_table(full_count, reduced):
    selected = jnp.arange(reduced)
    selected = jnp.where(selected <= reduced // 2, selected, selected + full_count - reduced)
    chosen = mode_table(full_count)[:, selected]
    product = jnp.dot(
        mode_table(reduced), chosen.T, precision=precise, preferred_element_type=jnp.float32
    )
    return jnp.sqrt(reduced / full_count) * product


def propagate(position_modes, momentum_modes, noise_modes):
    number = position_modes.shape[0]
    mode_index = jnp.arange(number)
    frequency = (
        2.0 * (number / INVERSE_TEMP) * jnp.sin(jnp.pi * mode_index.astype(jnp.float32) / number)
    )
    friction = jnp.where(mode_index == 0, CENTROID_FRICTION, 2.0 * frequency)
    damping = jnp.exp(-friction * TIME_STEP)
    kicking = jnp.sqrt((1.0 - damping * damping) / INVERSE_TEMP)
    cosine = jnp.cos(frequency * TIME_STEP)
    sine_term = jnp.sin(frequency * TIME_STEP)
    drift_factor = jnp.where(
        mode_index == 0, TIME_STEP, sine_term / jnp.where(mode_index == 0, 1.0, frequency)
    )
    spring = frequency * sine_term
    trailing = (number,) + (1,) * (position_modes.ndim - 1)
    damping = damping.reshape(trailing)
    kicking = kicking.reshape(trailing)
    cosine = cosine.reshape(trailing)
    drift_factor = drift_factor.reshape(trailing)
    spring = spring.reshape(trailing)
    momentum = damping * momentum_modes + kicking * noise_modes
    next_position = cosine * position_modes + drift_factor * momentum
    next_momentum = cosine * momentum - spring * position_modes
    return (next_position, next_momentum)


def atom_table(atom_types, occupancy, type_sigma, type_eps, type_mass):
    type_codes = jnp.arange(type_sigma.shape[0])
    onehot = (atom_types[..., None] == type_codes).astype(jnp.float32)
    sigma_atom = jnp.sum(onehot * type_sigma, -1)
    energy_root = jnp.sqrt(jnp.sum(onehot * type_eps, -1))
    mass_atom = jnp.sum(onehot * type_mass, -1)
    slot_index = jnp.arange(atom_types.shape[-1])
    living = (slot_index[None, :] < occupancy[:, None]).astype(jnp.float32)
    return (jnp.stack([sigma_atom, energy_root, living], 1), mass_atom)


def anchor_of(ext_index, domain_cells, slab_depth):
    slab_layer = ext_index // domain_cells - 1
    within = ext_index % domain_cells
    return jnp.stack([slab_layer, within // slab_depth, within % slab_depth], -1).astype(
        jnp.float32
    )


def taper(radius_sq, cutoff):
    margin = jnp.maximum(0.0, 1.0 - radius_sq / (cutoff * cutoff))
    return (margin * margin, -2.0 * margin / (cutoff * cutoff))


def pair_force(left_position, left_param, right_position, right_param, longer):
    separation = left_position[:, :, None] - right_position[:, None, :]
    radius_sq = jnp.sum(separation * separation, 0)
    sigma_pair = 0.5 * (left_param[0][:, None] + right_param[0][None, :])
    sigma_sq = sigma_pair * sigma_pair
    energy = left_param[1][:, None] * right_param[1][None, :]
    shifted = radius_sq + sigma_sq
    quotient = sigma_sq / shifted
    sixth_power = quotient * quotient * quotient
    potential = 4.0 * energy * (sixth_power * sixth_power - sixth_power)
    derivative = -12.0 * energy * (2.0 * sixth_power - 1.0) * sixth_power / shifted
    outer_value, outer_slope = taper(radius_sq, OUTER_CUT)
    inner_value, inner_slope = taper(radius_sq, INNER_CUT)
    if longer:
        switch = outer_value - inner_value
        switch_slope = outer_slope - inner_slope
    else:
        switch = inner_value
        switch_slope = inner_slope
    weight = -2.0 * (derivative * switch + potential * switch_slope)
    weight = weight * left_param[2][:, None] * right_param[2][None, :]
    return jnp.sum(weight[None] * separation, 2)


def row_force(absolute, ext_params, listing_table, bead_pick, cell_pick, longer):
    domain_cells = listing_table.shape[0]
    listing = listing_table[cell_pick]
    left_position = absolute[bead_pick, cell_pick + domain_cells]
    left_param = ext_params[cell_pick + domain_cells]
    right_position = jnp.transpose(absolute[bead_pick][listing], (1, 0, 2)).reshape(3, -1)
    right_param = jnp.transpose(ext_params[listing], (1, 0, 2)).reshape(3, -1)
    return pair_force(left_position, left_param, right_position, right_param, longer)


def shards(positions, momenta, noise, atom_types, occupancy, type_sigma, type_eps, type_mass):
    local_beads = positions.shape[0]
    domain_cells = positions.shape[1]
    slot_count = positions.shape[3]
    bead_count = lax.axis_size("bead")
    bead_rank = lax.axis_index("bead")
    total_beads = local_beads * bead_count
    listing_table = stencil_table(domain_cells, domain_cells, GZ, GY)
    params, mass_atom = atom_table(atom_types, occupancy, type_sigma, type_eps, type_mass)
    root_mass = jnp.sqrt(mass_atom)[None, :, None, :]
    ext_anchor = anchor_of(jnp.arange(3 * domain_cells + 1), domain_cells, GZ)[None, :, :, None]
    stacked = jnp.concatenate([positions, params[None]], 0)
    widened = with_halo(stacked, (("space", 1),), domain_cells)
    widened = jnp.concatenate([widened, jnp.zeros_like(widened[:, :1])], 1)
    absolute = widened[:-1] + ext_anchor
    ext_params = widened[-1]

    def short_row(row_index):
        return row_force(
            absolute,
            ext_params,
            listing_table,
            row_index // domain_cells,
            row_index % domain_cells,
            False,
        )

    short_force = lax.map(short_row, jnp.arange(local_beads * domain_cells)).reshape(
        positions.shape
    )
    kicked = momenta + 0.5 * TIME_STEP * short_force
    scaled_position = positions * root_mass
    scaled_momentum = kicked / root_mass
    matrix = mode_table(total_beads)
    pieces = domain_cells * 3 * slot_count // bead_count
    shaped = (
        scaled_position.reshape(local_beads, bead_count, pieces),
        scaled_momentum.reshape(local_beads, bead_count, pieces),
        noise.reshape(local_beads, bead_count, pieces),
    )
    position_modes = jnp.einsum(
        "kn,kij->nij",
        matrix,
        lax.all_to_all(shaped[0], "bead", split_axis=1, concat_axis=0, tiled=True),
        precision=precise,
    )
    momentum_modes = jnp.einsum(
        "kn,kij->nij",
        matrix,
        lax.all_to_all(shaped[1], "bead", split_axis=1, concat_axis=0, tiled=True),
        precision=precise,
    )
    noise_modes = jnp.einsum(
        "kn,kij->nij",
        matrix,
        lax.all_to_all(shaped[2], "bead", split_axis=1, concat_axis=0, tiled=True),
        precision=precise,
    )
    moved_position, moved_momentum = propagate(position_modes, momentum_modes, noise_modes)
    back_position = jnp.einsum("kn,nij->kij", matrix, moved_position, precision=precise)
    back_momentum = jnp.einsum("kn,nij->kij", matrix, moved_momentum, precision=precise)
    moved_x = lax.all_to_all(back_position, "bead", split_axis=0, concat_axis=1, tiled=True)
    moved_p = lax.all_to_all(back_momentum, "bead", split_axis=0, concat_axis=1, tiled=True)
    bead_position = moved_x.reshape(positions.shape)
    bead_momentum = moved_p.reshape(positions.shape)
    new_positions = bead_position / root_mass
    free_momenta = bead_momentum * root_mass
    weights = contract_table(total_beads, PC)
    reduced = weights.shape[0]
    held_groups = max(1, reduced // bead_count)
    row_total = reduced * domain_cells // bead_count
    cell_span = row_total // held_groups
    first_group = bead_rank * reduced // bead_count
    first_cell = bead_rank * row_total % domain_cells
    own_columns = lax.dynamic_slice_in_dim(weights, bead_rank * local_beads, local_beads, 1)
    chosen_rows = lax.dynamic_slice_in_dim(weights, first_group, held_groups, 0)
    chosen = jnp.einsum(
        "rk,kcda->rcda",
        chosen_rows,
        lax.all_gather(new_positions, "bead", axis=0, tiled=True),
        precision=precise,
    )
    stacked_slow = jnp.concatenate([chosen, params[None]], 0)
    widened_slow = with_halo(stacked_slow, (("space", 1),), domain_cells)
    widened_slow = jnp.concatenate([widened_slow, jnp.zeros_like(widened_slow[:, :1])], 1)
    absolute_slow = widened_slow[:-1] + ext_anchor
    params_slow = widened_slow[-1]

    def slow_row(row_index):
        return row_force(
            absolute_slow,
            params_slow,
            listing_table,
            row_index // cell_span,
            first_cell + row_index % cell_span,
            True,
        )

    slow_rows = lax.map(slow_row, jnp.arange(row_total))
    own_weights = own_columns.T
    arrived = lax.all_gather(slow_rows, "bead", axis=0, tiled=True)
    number = arrived.shape[0]
    global_rows = jnp.arange(number)
    group_hot = (global_rows[None, :] // domain_cells == jnp.arange(reduced)[:, None]).astype(
        jnp.float32
    )
    cell_hot = (global_rows[None, :] % domain_cells == jnp.arange(domain_cells)[:, None]).astype(
        jnp.float32
    )
    coeffs = jnp.dot(own_weights, group_hot, precision=precise, preferred_element_type=jnp.float32)
    mixing = (coeffs[:, None, :] * cell_hot[None]).reshape(local_beads * domain_cells, number)
    slow_total = jnp.dot(
        mixing, arrived.reshape(number, -1), precision=precise, preferred_element_type=jnp.float32
    )
    spread_force = total_beads / reduced * slow_total.reshape(positions.shape)
    new_momenta = free_momenta + 0.5 * TIME_STEP * spread_force
    return (new_positions, new_momenta)


def solution(mesh):
    placed = (
        P("bead", "space", None, None),
        P("bead", "space", None, None),
        P("bead", "space", None, None),
        P("space", None),
        P("space"),
        P(),
        P(),
        P(),
    )
    return jax.shard_map(
        shards,
        mesh=mesh,
        in_specs=placed,
        out_specs=(P("bead", "space", None, None), P("bead", "space", None, None)),
        check_vma=False,
    )
```

profile of v0, /device:TPU:0, one launch (start us, length us, event | category | flops | bytes accessed | tf_op | source)
XLA Modules:
  0.0 780.9 jit_solution(12978386404767101330)
XLA Ops:
  3.7 2.0 collective-permute-start.1
  7.4 6.5 all-to-all-start.2
  15.7 529.9 %while.24 = (s32[]{:T(128)}, f32[64,3,128]{2,0,1:T(8,128)S(1)}, s32[64]{0:T(128)S(1)}, f32[49,3,128]{2,1,0:T(4,128)S(1)}, s32[16,27]{1,0:T(8,128)S(1)}, /*index=...) while((s32[]{:T(128)}, f32[64,3,128]{2,0,1:T(8,128)S(1)}, ...), condition=%wide.region_6.7_spmd, body=%wide.region_3.6_spmd.sunk | while | flops 19907440 | bytes 7628254 | solution.py:184
  21.3 1.8 fusion.117
  29.6 1.8 fusion.117
  71.0 1.8 fusion.117
  79.3 1.8 fusion.117
  87.6 1.8 fusion.117
  104.1 1.8 fusion.117
  112.4 1.8 fusion.117
  153.8 1.8 fusion.117
  162.1 1.8 fusion.117
  170.4 1.8 fusion.117
  195.2 1.8 fusion.117
  203.5 1.8 fusion.117
  211.8 1.8 fusion.117
  220.0 1.8 fusion.117
  236.6 1.8 fusion.117
  244.9 1.8 fusion.117
  269.7 1.8 fusion.117
  278.0 1.8 fusion.117
  286.3 1.8 fusion.117
  294.6 1.8 fusion.117
  302.8 1.8 fusion.117
  327.7 1.8 fusion.117
  360.8 1.8 fusion.117
  369.1 1.8 fusion.117
  377.3 1.8 fusion.117
  385.6 1.8 fusion.117
  393.9 1.8 fusion.117
  402.2 1.8 fusion.117
  410.5 1.8 fusion.117
  435.3 1.8 fusion.117
  443.6 1.8 fusion.117
  451.9 1.8 fusion.117
  460.1 1.8 fusion.117
  493.2 1.8 fusion.117
  501.5 1.8 fusion.117
  546.4 6.0 all-to-all-start.1
  553.5 6.1 all-to-all-done.1
  559.6 3.4 all-to-all-start
  563.0 7.0 all-to-all-done
  572.1 3.4 all-to-all-start.3
  576.7 5.8 all-to-all-done.3
  582.5 3.4 all-to-all-start.4
  586.0 32.7 %all_gather.6 = f32[32,16,3,128]{3,1,2,0:T(8,128)S(1)} all-gather(f32[4,16,3,128]{3,1,2,0:T(8,128)S(1)} %copy_divide_fusion), channel_id=1, replica_groups=mesh['bead'=8,'space'=4] {'bead'}, dimensions={0}, use_global_device_ids=true | all-gather | bytes 884736 | tf_op jit(solution)/shard_map/all_gather | solution.py:236
  623.3 125.8 %while.25 = (s32[]{:T(128)}, f32[16,3,128]{2,0,1:T(8,128)S(1)}, s32[16]{0:T(128)S(1)}, s32[]{:T(128)}, f32[49,3,128]{2,1,0:T(4,128)S(1)}, /*index=5*/s32[16,27]{...) while((s32[]{:T(128)}, f32[16,3,128]{2,0,1:T(8,128)S(1)}, ...), condition=%wide.region_10.11_spmd, body=%wide.region_7.10_spmd.sunk | while | flops 22561636 | bytes 7477610 | solution.py:255
  628.3 2.1 fusion.121
  636.1 2.1 fusion.121
  644.0 2.1 fusion.121
  651.8 2.1 fusion.121
  659.7 2.1 fusion.121
  667.6 2.1 fusion.121
  675.4 2.1 fusion.121
  683.3 2.1 fusion.121
  691.1 2.1 fusion.121
  699.0 2.1 fusion.121
  706.9 2.1 fusion.121
  714.7 2.1 fusion.121
  722.6 2.1 fusion.121
  730.4 2.1 fusion.121
  738.3 2.1 fusion.121
  746.2 2.1 fusion.121
  749.1 30.6 %all_gather.7 = f32[128,3,128]{2,0,1:T(8,128)S(1)} all-gather(f32[16,3,128]{2,0,1:T(8,128)S(1)} %get-tuple-element.179), channel_id=1, replica_groups=mesh['bead'=8,'space'=4] {'bead'}, dimensions={0}, use_global_device_ids=true | all-gather | bytes 221184 | tf_op jit(solution)/shard_map/all_gather | solution.py:257
  (1224 shorter events, 354.2 us)
Async XLA Ops:
  3.2 12.2 %collective-permute-start = (f32[5,16,3,128]{3,2,1,0:T(4,128)S(1)}, f32[5,16,3,128]{3,2,1,0:T(4,128)S(1)}, u32[]{:S(2)}, u32[]{:S(2)}) collective-permute-start(f32[5,16,3,128]{3,2,1,0:T(4,128)S(1)} %copy_dynamic-update-slice_fusion.1), channel_id=1, source_target_pairs={{0,1},{1,2},{2,3},{3,0},{4,5},{5,6},{6,7},{7,4},{8,9},{9,10},{10,1... | collective-permute-start | bytes 368648 | tf_op jit(solution)/shard_map/ppermute | solution.py:26
  3.7 11.7 %collective-permute-start.1 = (f32[5,16,3,128]{3,2,1,0:T(4,128)S(1)}, f32[5,16,3,128]{3,2,1,0:T(4,128)S(1)}, u32[]{:S(2)}, u32[]{:S(2)}) collective-permute-start(f32[5,16,3,128]{3,2,1,0:T(4,128)S(1)} %copy_dynamic-update-slice_fusion.1), channel_id=1, source_target_pairs={{1,0},{2,1},{3,2},{0,3},{5,4},{6,5},{7,6},{4,7},{9,8},{10,9},{11,1... | collective-permute-start | bytes 368648 | tf_op jit(solution)/shard_map/ppermute | solution.py:28
  7.4 539.1 %all-to-all-start.2 = ((f32[4,8,768]{2,0,1:T(4,128)}), f32[4,8,768]{2,0,1:T(4,128)S(1)}, u32[]{:S(2)}, u32[]{:S(2)}) async-start(f32[4,8,768]{2,0,1:T(4,128)} %copy.55), calls=%async_computation.2 | async-start | bytes 196608 | tf_op jit(solution)/shard_map/all_to_all | solution.py:212
  15.7 529.9 %copy-start.1 = (f32[4,16,3,128]{3,1,2,0:T(8,128)S(1)}, f32[4,16,3,128]{3,1,2,0:T(8,128)}, u32[]{:S(2)}) copy-start(f32[4,16,3,128]{3,1,2,0:T(8,128)} %param.12) | copy-start | bytes 294916
  15.7 529.9 %copy-start.2 = (f32[4,16,3,128]{3,1,2,0:T(8,128)S(1)}, f32[4,16,3,128]{3,1,2,0:T(8,128)}, u32[]{:S(2)}) copy-start(f32[4,16,3,128]{3,1,2,0:T(8,128)} %param.13) | copy-start | bytes 294916
  546.4 13.1 %all-to-all-start.1 = ((f32[4,8,768]{2,0,1:T(4,128)}), f32[4,8,768]{2,0,1:T(4,128)S(1)}, u32[]{:S(2)}, u32[]{:S(2)}) async-start(f32[4,8,768]{2,0,1:T(4,128)} %copy.53), calls=%async_computation.1 | async-start | bytes 196608 | tf_op jit(solution)/shard_map/all_to_all | solution.py:206
  559.6 10.4 %all-to-all-start = ((f32[4,8,768]{2,0,1:T(4,128)}), f32[4,8,768]{2,0,1:T(4,128)S(1)}, u32[]{:S(2)}, u32[]{:S(2)}) async-start(f32[4,8,768]{2,0,1:T(4,128)} %copy.46), calls=%async_computation | async-start | bytes 196608 | tf_op jit(solution)/shard_map/all_to_all | solution.py:200
  572.1 10.4 %all-to-all-start.3 = ((f32[32,1,768]{2,1,0:T(1,128)}), f32[32,1,768]{2,1,0:T(1,128)S(1)}, u32[]{:S(2)}, u32[]{:S(2)}) async-start(f32[32,1,768]{2,1,0:T(1,128)} %copy.56), calls=%async_computation.3 | async-start | bytes 196608 | tf_op jit(solution)/shard_map/all_to_all | solution.py:218
  582.5 39.0 %all-to-all-start.4 = ((f32[32,1,768]{2,1,0:T(1,128)}), f32[32,1,768]{2,1,0:T(1,128)S(1)}, u32[]{:S(2)}, u32[]{:S(2)}) async-start(f32[32,1,768]{2,1,0:T(1,128)} %copy.59), calls=%async_computation.4 | async-start | bytes 196608 | tf_op jit(solution)/shard_map/all_to_all | solution.py:219
  586.0 37.3 %copy-start = (f32[4,16,3,128]{3,1,2,0:T(8,128)}, f32[4,16,3,128]{3,1,2,0:T(8,128)S(1)}, u32[]{:S(2)}) copy-start(f32[4,16,3,128]{3,1,2,0:T(8,128)S(1)} %copy_divide_fusion) | copy-start | bytes 294916
  619.5 3.6 collective-permute-start.2
  619.6 3.5 collective-permute-start.3
where the time goes:
time: 787 us; the launch traced here: 781 us
  other arithmetic  273 us (35%)
  loops' own time  220 us (28%)
  local copies, waits for them, and re-layouts  173 us (22%)
  blocking collectives  63.4 us (8%)
  starting transfers between devices  26.9 us (3%)
  waiting for transfers between devices  20.3 us (3%)
    another operation x1, loops' own time, shards(): lax.map(short_row, jnp.arange(local_beads * domain_cells))  185 us
    mul x80, other arithmetic, pair_force(): weight = weight * left_param[2][:, None] * right_param[2][None, :]  152 us
    reduce_sum x80, other arithmetic, pair_force(): radius_sq = jnp.sum(separation * separation, 0)  58.6 us
    reduce_sum x80, other arithmetic, pair_force(): return jnp.sum(weight[None] * separation, 2)  57.4 us
    gather x80, local copies, waits for them, and re-layouts, row_force(): right_param = jnp.transpose(ext_params[listing], (1, 0, 2)).reshape(3, -1)  48.2 us
    gather x80, local copies, waits for them, and re-layouts, row_force(): absolute[bead_pick][listing]  48.2 us
    dynamic_slice x64, local copies, waits for them, and re-layouts, shards(): lax.map(short_row, jnp.arange(local_beads * domain_cells))  42.6 us
    another operation x1, loops' own time, shards(): slow_rows = lax.map(slow_row, jnp.arange(row_total))  35 us
  transfers between devices with their start and end apart: 9, of which 4 were waited for; matrix products, arithmetic and copies ran while one was open for 45% of the time, Pallas kernels for 0%

commit v1 on v0

v1 whole, which is shorter than its diff:
```python
import functools

import jax
import jax.numpy as jnp
import numpy as np
from jax import lax
from jax.experimental import pallas as pl
from jax.experimental.pallas import tpu as pltpu
from jax.sharding import PartitionSpec as P

PC = 8
GY = 4
GZ = 4

TIME_STEP = 0.05
INVERSE_TEMP = 32.0
CENTROID_FRICTION = 1.0
INNER_CUT = 0.5
OUTER_CUT = 1.0
CUBE_ROOT_TWO = 2.0 ** (1.0 / 3.0)
F32 = jnp.float32
BF16 = jnp.bfloat16
VMEM_LIMIT = 48 * 1024 * 1024


def mode_matrix(number):
    rows = np.arange(number, dtype=np.float64)[:, None]
    column = np.arange(number, dtype=np.float64)[None, :]
    phases = 2.0 * np.pi * rows * column / number
    factor = np.sqrt(2.0 / number)
    middle = np.cos(np.pi * rows) / np.sqrt(number)
    matrix = np.where(column < number / 2, factor * np.cos(phases), factor * np.sin(phases))
    matrix = np.where(column == number / 2, middle, matrix)
    return np.where(column == 0, 1.0 / np.sqrt(number), matrix)


def contract_matrix(full_count, reduced):
    selected = np.arange(reduced)
    selected = np.where(selected <= reduced // 2, selected, selected + full_count - reduced)
    chosen = mode_matrix(full_count)[:, selected]
    return np.sqrt(reduced / full_count) * (mode_matrix(reduced) @ chosen.T)


def step_matrices(number):
    index = np.arange(number, dtype=np.float64)
    frequency = 2.0 * (number / INVERSE_TEMP) * np.sin(np.pi * index / number)
    friction = np.where(index == 0, CENTROID_FRICTION, 2.0 * frequency)
    damping = np.exp(-friction * TIME_STEP)
    kicking = np.sqrt((1.0 - damping * damping) / INVERSE_TEMP)
    cosine = np.cos(frequency * TIME_STEP)
    sine = np.sin(frequency * TIME_STEP)
    drift = np.where(index == 0, TIME_STEP, sine / np.where(index == 0, 1.0, frequency))
    modes = mode_matrix(number)

    def over_beads(diagonal):
        return (modes * diagonal[None, :]) @ modes.T

    return np.array(
        [
            [over_beads(cosine), over_beads(drift * damping), over_beads(drift * kicking)],
            [
                over_beads(-frequency * sine),
                over_beads(cosine * damping),
                over_beads(cosine * kicking),
            ],
        ]
    )


def cell_pairs(domain_cells):
    inside, across = [], []
    for one in range(domain_cells):
        for two in range(domain_cells):
            if abs(one // GZ - two // GZ) <= 1 and abs(one % GZ - two % GZ) <= 1:
                across.append((one, two))
                if one < two:
                    inside.append((one, two))
    return np.array(inside, np.int32), np.array(across, np.int32)


def split_three(value):
    high = value.astype(BF16).astype(F32)
    rest = value - high
    middle = rest.astype(BF16).astype(F32)
    return high, middle, rest - middle


def dot(left, right, contract=((1,), (0,))):
    return lax.dot_general(left, right, (contract, ((), ())), preferred_element_type=F32)


def cell_vector(position, half_sigma, layer, cell):
    row = lax.broadcasted_iota(jnp.int32, (8, position.shape[-1]), 0)
    block = jnp.concatenate(
        [position, half_sigma, jnp.zeros((4, position.shape[-1]), F32)], axis=0
    )
    corner = jnp.where(
        row == 0,
        float(layer - 1),
        jnp.where(
            row == 1,
            (cell // GZ).astype(F32) - GY / 2,
            jnp.where(row == 2, (cell % GZ).astype(F32) - GZ / 2, 0.0),
        ),
    )
    return block + corner, row


def right_side(vector, row):
    norm = jnp.sum(vector * vector, axis=0, keepdims=True)
    full = jnp.where(row == 4, norm, jnp.where(row == 5, 1.0, vector))
    high, middle, low = split_three(full)
    return jnp.concatenate([high, middle, high, low, high, middle], axis=0)


def left_side(vector, row):
    norm = jnp.sum(vector * vector, axis=0, keepdims=True)
    full = jnp.where(
        row < 3,
        -2.0 * vector,
        jnp.where(
            row == 3, 2.0 * vector, jnp.where(row == 4, 1.0, jnp.where(row == 5, norm, 0.0))
        ),
    )
    high, middle, low = split_three(full)
    return jnp.concatenate([high, high, middle, high, low, middle], axis=0)


def source_rows(vector, row, strength):
    full = strength * jnp.where(row == 3, 1.0, vector)
    high, middle, low = split_three(full)
    return jnp.concatenate([high, middle, low, jnp.zeros_like(low)], axis=0)


def pair_weight(h, s2, longer):
    guess = pl.reciprocal(h, approx=True)
    inverse = guess * (2.0 - h * guess)
    if longer:
        quotient = s2 * inverse
        sixth = quotient * quotient * quotient
        radius_sq = h - s2
        outer = jnp.maximum(1.0 - radius_sq, 0.0)
        inner = jnp.maximum(1.0 - 4.0 * radius_sq, 0.0)
        switch = outer * outer - inner * inner
        slope = outer - 4.0 * inner
        return sixth * (
            (6.0 * sixth - 3.0) * (switch * inverse) + (2.0 * sixth - 2.0) * slope
        )
    scaled, reach = s2
    quotient = scaled * inverse
    twice = quotient * quotient * quotient
    edge = jnp.maximum(reach * inverse - 1.0, 2.0)
    bracket = edge * (twice - 1.0) - twice
    return (twice * bracket) * ((edge - 2.0) * h)


def pair_block(left, right, source_left, source_right, s2, longer, reaction):
    h = dot(left, right)
    chunk = 32
    highs, lows = [], []
    for start in range(0, h.shape[0], chunk):
        piece = slice(start, start + chunk)
        if longer:
            terms = s2[piece]
        else:
            terms = (s2[0][piece], s2[1][piece])
        weight = pair_weight(h[piece], terms, longer)
        high = weight.astype(BF16)
        highs.append(high)
        lows.append((weight - high.astype(F32)).astype(BF16))
    high = jnp.concatenate(highs, axis=0)
    low = jnp.concatenate(lows, axis=0)

    def fold(total):
        return total[0:8] + total[8:16] + total[16:24]

    on_right = fold(dot(source_left, high) + dot(source_left, low))
    if not reaction:
        return on_right, None
    across = ((1,), (1,))
    on_left = fold(dot(source_right, high, across) + dot(source_right, low, across))
    return on_right, on_left


def size_terms(s2, longer):
    if longer:
        return s2
    return CUBE_ROOT_TWO * s2, 0.75 + 3.0 * s2


def force_of(total, vector, strength, factor):
    return (factor * strength) * (vector[0:3] * total[3:4] - total[0:3])


def weight_factor(longer):
    return 8.0 if longer else 64.0 / 3.0


def prepare(read, params, layer, beads, cells, left_ref, right_ref, source_ref, size_left, size_right):
    lanes = params.shape[-1]

    def one(bead, cell):
        half_sigma = params[cell, 0:1, :]
        strength = params[cell, 1:2, :]
        vector, row = cell_vector(read(bead, cell), half_sigma, layer, cell)
        if left_ref is not None:
            left_ref[bead, cell] = left_side(vector, row).T.astype(BF16)
        if right_ref is not None:
            right_ref[bead, cell] = right_side(vector, row).astype(BF16)
        source_ref[bead, cell] = source_rows(vector, row, strength).astype(BF16)

    def sizes(cell):
        half_sigma = params[cell, 0:1, :]
        row = lax.broadcasted_iota(jnp.int32, (8, lanes), 0)
        vector = jnp.where(row == 3, half_sigma, 0.0)
        if left_ref is not None:
            size_left[cell] = left_side(vector, row).T.astype(BF16)
        if right_ref is not None:
            size_right[cell] = right_side(vector, row).astype(BF16)

    def per_cell(cell, carry):
        sizes(cell)
        for bead in range(beads):
            one(bead, cell)
        return carry

    lax.fori_loop(0, cells, per_cell, 0)


def inside_kernel(longer, pairs_ref, position, params, total_ref, left_ref, right_ref, source_ref, size_left, size_right):
    beads, cells = position.shape[:2]
    prepare(
        lambda bead, cell: position[bead, cell],
        params,
        0,
        beads,
        cells,
        left_ref,
        right_ref,
        source_ref,
        size_left,
        size_right,
    )

    def own(cell, carry):
        s2 = size_terms(dot(size_left[cell], size_right[cell]), longer)
        for bead in range(beads):
            source = source_ref[bead, cell]
            total, _ = pair_block(
                left_ref[bead, cell], right_ref[bead, cell], source, source, s2, longer, False
            )
            total_ref[bead, cell] = total
        return carry

    lax.fori_loop(0, cells, own, 0)

    def pair(index, carry):
        one = pairs_ref[index, 0]
        two = pairs_ref[index, 1]
        s2 = size_terms(dot(size_left[one], size_right[two]), longer)
        for bead in range(beads):
            on_two, on_one = pair_block(
                left_ref[bead, one],
                right_ref[bead, two],
                source_ref[bead, one],
                source_ref[bead, two],
                s2,
                longer,
                True,
            )
            total_ref[bead, two] += on_two
            total_ref[bead, one] += on_one
        return carry

    lax.fori_loop(0, pairs_ref.shape[0], pair, 0)


def across_kernel(
    longer, pairs_ref, position, params, next_position, next_params, held, force_ref, back_ref,
    total_ref, next_total, left_ref, right_ref, source_ref, next_source, size_left, size_right,
):
    beads, cells = position.shape[:2]
    prepare(
        lambda bead, cell: position[bead, cell],
        params, 0, beads, cells, None, right_ref, source_ref, None, size_right,
    )
    prepare(
        lambda bead, cell: next_position[bead, cell],
        next_params, 1, beads, cells, left_ref, None, next_source, size_left, None,
    )
    total_ref[...] = held[...]
    next_total[...] = jnp.zeros_like(next_total)

    def pair(index, carry):
        one = pairs_ref[index, 0]
        two = pairs_ref[index, 1]
        s2 = size_terms(dot(size_left[one], size_right[two]), longer)
        for bead in range(beads):
            on_two, on_one = pair_block(
                left_ref[bead, one],
                right_ref[bead, two],
                next_source[bead, one],
                source_ref[bead, two],
                s2,
                longer,
                True,
            )
            total_ref[bead, two] += on_two
            next_total[bead, one] += on_one
        return carry

    lax.fori_loop(0, pairs_ref.shape[0], pair, 0)

    def finish(cell, carry):
        for bead in range(beads):
            for layer, place, values, total, out in (
                (0, position, params, total_ref, force_ref),
                (1, next_position, next_params, next_total, back_ref),
            ):
                vector, _ = cell_vector(place[bead, cell], values[cell, 0:1, :], layer, cell)
                out[bead, cell] = force_of(
                    total[bead, cell], vector, values[cell, 1:2, :], weight_factor(longer)
                )
        return carry

    lax.fori_loop(0, cells, finish, 0)


def call(kernel, inputs, smem, outputs, scratch, flops):
    return pl.pallas_call(
        kernel,
        out_shape=outputs,
        in_specs=[
            pl.BlockSpec(memory_space=pltpu.SMEM if place < smem else pltpu.VMEM)
            for place in range(len(inputs))
        ],
        scratch_shapes=scratch,
        compiler_params=pltpu.CompilerParams(vmem_limit_bytes=VMEM_LIMIT),
        cost_estimate=pl.CostEstimate(flops=flops, bytes_accessed=1 << 18, transcendentals=0),
    )(*inputs)


PAIR_FLOPS = 40 * 128 * 128


def pair_scratch(beads, cells, lanes):
    return dict(
        left=pltpu.VMEM((beads, cells, lanes, 48), BF16),
        right=pltpu.VMEM((beads, cells, 48, lanes), BF16),
        source=pltpu.VMEM((beads, cells, 32, lanes), BF16),
        size_left=pltpu.VMEM((cells, lanes, 48), BF16),
        size_right=pltpu.VMEM((cells, 48, lanes), BF16),
        total=pltpu.VMEM((beads, cells, 8, lanes), F32),
    )


def pair_forces(position, params, next_position, next_params, longer):
    beads, cells, _, lanes = position.shape
    inside, across = cell_pairs(cells)
    room = pair_scratch(beads, cells, lanes)
    held = call(
        functools.partial(inside_kernel, longer),
        (jnp.asarray(inside), position, params),
        1,
        jax.ShapeDtypeStruct((beads, cells, 8, lanes), F32),
        [room["left"], room["right"], room["source"], room["size_left"], room["size_right"]],
        PAIR_FLOPS * beads * (len(inside) + cells),
    )
    forces = jax.ShapeDtypeStruct((beads, cells, 3, lanes), F32)
    return call(
        functools.partial(across_kernel, longer),
        (jnp.asarray(across), position, params, next_position, next_params, held),
        1,
        (forces, forces),
        [
            room["total"], room["total"], room["left"], room["right"], room["source"],
            room["source"], room["size_left"], room["size_right"],
        ],
        PAIR_FLOPS * beads * len(across),
    )


def kick_kernel(
    piece_rows, groups, table, rank, position, momenta, noise, force, back, params, partial_ref, piece_ref
):
    beads, cells = position.shape[:2]
    holders = piece_ref.shape[0]
    reduced = table.shape[0]
    first = rank[0] * beads
    if holders * piece_rows > 3 * cells:
        piece_ref[...] = jnp.zeros_like(piece_ref)
    for cell in range(cells):
        mass = params[cell, 2:3, :]
        per_mass = 1.0 / mass
        per_root = lax.rsqrt(mass)
        per_root = per_root * (1.5 - 0.5 * mass * per_root * per_root)
        inputs = []
        for bead in range(beads):
            kicked = momenta[bead, cell] + 0.5 * TIME_STEP * (force[bead, cell] + back[bead, cell])
            inputs.append((position[bead, cell], kicked * per_mass, noise[bead, cell] * per_root))
        for bead in range(beads):
            for kind in range(3):
                base = (kind * beads + bead) * piece_rows
                if piece_rows % 3 == 0:
                    owner, row = divmod(3 * cell, piece_rows)
                    piece_ref[owner, base + row : base + row + 3, :] = inputs[bead][kind]
                else:
                    for axis in range(3):
                        owner, row = divmod(3 * cell + axis, piece_rows)
                        piece_ref[owner, base + row : base + row + 1, :] = inputs[bead][kind][
                            axis : axis + 1
                        ]
        for group in range(reduced):
            total = None
            for bead in range(beads):
                for kind in range(3):
                    term = table[group, kind * holders * beads + first + bead] * inputs[bead][kind]
                    total = term if total is None else total + term
            for copy in range(groups):
                partial_ref[group * groups + copy, 3 * cell : 3 * cell + 3, :] = total


def move_kernel(piece_rows, beads, matrix, arrived, out_ref, gathered):
    holders = arrived.shape[0]
    taken = 3 * beads
    given = 2 * beads
    for row in range(piece_rows):
        for holder in range(holders):
            gathered[row, holder * taken : (holder + 1) * taken, :] = arrived[
                holder, pl.ds(row, taken, stride=piece_rows), :
            ]
        moved = lax.dot_general(
            matrix[...],
            gathered[row],
            (((1,), (0,)), ((), ())),
            precision=lax.Precision.HIGHEST,
            preferred_element_type=F32,
        )
        for holder in range(holders):
            out_ref[holder, row * given : (row + 1) * given, :] = moved[
                holder * given : (holder + 1) * given
            ]


def finish_kernel(piece_rows, groups, table, rank, moved, slow, params, position_ref, momentum_ref):
    beads, cells = position_ref.shape[:2]
    given = 2 * beads
    reduced = table.shape[0]
    first = rank[0] * beads
    for cell in range(cells):
        mass = params[cell, 2:3, :]
        for bead in range(beads):
            def taken(kind):
                if piece_rows % 3 == 0:
                    owner, row = divmod(3 * cell, piece_rows)
                    return moved[owner, pl.ds(row * given + kind * beads + bead, 3, stride=given), :]
                rows = []
                for axis in range(3):
                    owner, row = divmod(3 * cell + axis, piece_rows)
                    place = row * given + kind * beads + bead
                    rows.append(moved[owner, place : place + 1, :])
                return jnp.concatenate(rows, axis=0)

            position_ref[bead, cell] = taken(0)
            total = mass * taken(1)
            for group in range(reduced):
                total = total + table[group, first + bead] * slow[
                    group * groups, 3 * cell : 3 * cell + 3, :
                ]
            momentum_ref[bead, cell] = total


def shards(positions, momenta, noise, atom_types, occupancy, type_sigma, type_eps, type_mass):
    beads, cells, _, lanes = positions.shape
    holders = lax.axis_size("bead")
    domains = lax.axis_size("space")
    rank = lax.axis_index("bead")
    total_beads = beads * holders
    rows = 3 * cells
    piece_rows = -(-rows // holders)
    held = max(1, PC // holders)
    groups = max(1, holders // PC)
    contract = contract_matrix(total_beads, PC)
    steps = step_matrices(total_beads)
    rank_table = rank.astype(jnp.int32).reshape(1)
    one_back = [((i + 1) % domains, i) for i in range(domains)]
    one_on = [(i, (i + 1) % domains) for i in range(domains)]

    codes = jnp.arange(type_sigma.shape[0])
    onehot = atom_types[..., None] == codes
    living = jnp.arange(lanes)[None, :] < occupancy[:, None]
    half_sigma = 0.5 * jnp.sum(jnp.where(onehot, type_sigma, 0.0), -1)
    root_eps = jnp.sqrt(jnp.sum(jnp.where(onehot, type_eps, 0.0), -1))
    mass = jnp.sum(jnp.where(onehot, type_mass, 0.0), -1)
    params = jnp.stack([half_sigma, jnp.where(living, root_eps, 0.0), mass], 1)

    stacked = jnp.concatenate([positions, params[None]], 0)
    next_stacked = lax.ppermute(stacked, "space", one_back)
    next_params = next_stacked[beads]
    force, back = pair_forces(positions, params, next_stacked[:beads], next_params, False)
    back = lax.ppermute(back, "space", one_on)

    position_map = np.concatenate([contract @ steps[0, kind] for kind in range(3)], axis=1)
    partial, pieces = call(
        functools.partial(kick_kernel, piece_rows, groups),
        (
            jnp.asarray(position_map, F32), rank_table, positions, momenta, noise, force, back,
            params,
        ),
        2,
        (
            jax.ShapeDtypeStruct((PC * groups, rows, lanes), F32),
            jax.ShapeDtypeStruct((holders, 3 * beads * piece_rows, lanes), F32),
        ),
        [],
        1 << 22,
    )
    arrived = lax.all_to_all(
        partial.reshape(holders, held * rows, lanes), "bead", split_axis=0, concat_axis=0, tiled=True
    )
    contracted = jnp.sum(arrived, 0).reshape(held, cells, 3, lanes)
    next_contracted = lax.ppermute(contracted, "space", one_back)
    pieces = lax.all_to_all(pieces, "bead", split_axis=0, concat_axis=0, tiled=True)
    slow, slow_back = pair_forces(contracted, params, next_contracted, next_params, True)
    slow = slow + lax.ppermute(slow_back, "space", one_on)

    order = steps.reshape(2, 3, holders, beads, holders, beads).transpose(2, 0, 3, 4, 1, 5)
    order = order.reshape(2 * total_beads, 3 * total_beads)
    moved = call(
        functools.partial(move_kernel, piece_rows, beads),
        (jnp.asarray(order, F32), pieces),
        0,
        jax.ShapeDtypeStruct((holders, 2 * beads * piece_rows, lanes), F32),
        [pltpu.VMEM((piece_rows, 3 * total_beads, lanes), F32)],
        1 << 23,
    )
    moved_rows = 2 * beads * piece_rows
    sent = jnp.concatenate(
        [
            moved,
            jnp.broadcast_to(slow.reshape(1, held * rows, lanes), (holders, held * rows, lanes)),
        ],
        1,
    )
    got = lax.all_to_all(sent, "bead", split_axis=0, concat_axis=0, tiled=True)
    spread = 0.5 * TIME_STEP * (total_beads / PC) * contract
    shape = jax.ShapeDtypeStruct(positions.shape, F32)
    return call(
        functools.partial(finish_kernel, piece_rows, groups),
        (
            jnp.asarray(spread, F32), rank_table, got[:, :moved_rows],
            got[:, moved_rows:].reshape(holders * held, rows, lanes), params,
        ),
        2,
        (shape, shape),
        [],
        1 << 20,
    )


def solution(mesh):
    placed = (
        P("bead", "space", None, None),
        P("bead", "space", None, None),
        P("bead", "space", None, None),
        P("space", None),
        P("space"),
        P(),
        P(),
        P(),
    )
    return jax.shard_map(
        shards,
        mesh=mesh,
        in_specs=placed,
        out_specs=(P("bead", "space", None, None), P("bead", "space", None, None)),
        check_vma=False,
    )
```

time: 787 us -> 284 us (0.36)
  other arithmetic: 273 us -> 1 us
  Pallas kernels: 0 us -> 232 us
  loops' own time: 220 us -> 0 us
  local copies, waits for them, and re-layouts: 173 us -> 6.11 us
  blocking collectives: 63.4 us -> 30.3 us
  starting transfers between devices: 26.9 us -> 6.54 us
  waiting for transfers between devices: 20.3 us -> 6.3 us
    pallas_call x0 -> x7, Pallas kernels: none -> 232 us  [call(): pl.pallas_call(kernel, out_shape=outputs, in_specs=[pl.BlockSpec(memory_s...]
    another operation x2 -> x0, loops' own time: 220 us -> none  [the longest x1 185 us: shards(): lax.map(short_row, jnp.arange(local_beads * domain_cells))]
    mul x166 -> x1, other arithmetic: 153 us -> 0.01 us  [shards(): half_sigma = 0.5 * jnp.sum(jnp.where(onehot, type_sigma, 0.0), -1)]
    reduce_sum x161 -> x2, other arithmetic: 117 us -> 0.8 us  [the longest x1 0.78 us: shards(): half_sigma = 0.5 * jnp.sum(jnp.where(onehot, type_sigma, 0.0), -1)]
    gather x161 -> x0, local copies, waits for them, and re-layouts: 97 us -> none  [the longest x80 48.2 us: row_force(): right_param = jnp.transpose(ext_params[listing], (1, 0, 2)).reshape(3, -1)]
    all_gather x2 -> x0, blocking collectives: 63.4 us -> none  [the longest x1 32.7 us: shards(): lax.all_gather(new_positions, 'bead', axis=0, tiled=True)]
    dynamic_slice x160 -> x0, local copies, waits for them, and re-layouts: 54.1 us -> none  [the longest x64 42.6 us: shards(): lax.map(short_row, jnp.arange(local_beads * domain_cells))]
    all_to_all x0 -> x2, blocking collectives: none -> 30.3 us  [the longest x1 16.9 us: shards(): got = lax.all_to_all(sent, 'bead', split_axis=0, concat_axis=0, tiled=True)]
  transfers between devices with their start and end apart: 9 -> 5, of which waited for: 4 -> 2; matrix products, arithmetic and copies ran while one was open for 45% -> 0% of each run, Pallas kernels for 0% -> 43%
where the time goes in v1:
time: 284 us
  Pallas kernels  232 us (82%)
  blocking collectives  30.3 us (11%)
  starting transfers between devices  6.54 us (2%)
  waiting for transfers between devices  6.3 us (2%)
  local copies, waits for them, and re-layouts  6.11 us (2%)
    pallas_call x7, Pallas kernels, call(): pl.pallas_call(kernel, out_shape=outputs, in_specs=[pl.BlockSpec(memory_s...  232 us
    all_to_all x1, blocking collectives, shards(): got = lax.all_to_all(sent, 'bead', split_axis=0, concat_axis=0, tiled=True)  16.9 us
    all_to_all x1, blocking collectives, shards(): lax.all_to_all(partial.reshape(holders, held * rows, lanes), 'bead', spli...  13.4 us
  transfers between devices with their start and end apart: 5, of which 2 were waited for; matrix products, arithmetic and copies ran while one was open for 0% of the time, Pallas kernels for 43%

profile of v1, /device:TPU:0, one launch (start us, length us, event | category | flops | bytes accessed | tf_op | source)
XLA Modules:
  0.0 283.5 jit_solution(12845032272120385882)
XLA Ops:
  0.6 0.8 select_reduce_fusion.2
  1.4 0.9 copy.36.position
  2.4 0.0 copy-start.7
  2.4 0.6 copy-done.7
  3.1 0.1 compare_select_fusion
  3.2 0.0 copy-start.2
  3.2 2.5 collective-permute-start
  5.7 0.0 copy-done.2
  5.7 59.4 %shard_map.158.held = f32[4,16,8,128]{3,2,1,0:T(8,128)S(1)} custom-call(s32[42,2]{1,0:T(8,128)S(1)} %copy-done.2, f32[4,16,3,128]{3,2,1,0:T(4,128)S(1)} %copy.36.position, f32[16,3,128]{2,1,0:T(4,128)S(1)} %get-tuple-element.26.params), custom_call_target="tpu_custom_call" | custom-call | flops 152043520 | bytes 262144 | tf_op jit(solution)/shard_map/pallas_call | solution.py:330
  65.1 0.0 collective-permute-done
  65.2 0.0 copy-start
  65.2 0.8 copy-done
  66.0 0.0 copy-start.5
  66.0 105.5 %shard_map.159 = (f32[4,16,3,128]{3,2,1,0:T(4,128)S(1)}, f32[4,16,3,128]{3,2,1,0:T(4,128)S(1)}) custom-call(s32[100,2]{1,0:T(8,128)S(1)} %copy-done, f32[4,16,3,128]{3,2,1,0:T(4,128)S(1)} %copy.36.position, f32[16,3,128]{2,1,0:T(4,128)S(1)} %get-tuple-element.26.params, f32[4,16,3,128]{3,2,1,0:T(4,128)S(1)} %slice.16.next_position, ...), custom_call_target="tpu_custom_call" | custom-call | flops 262144000 | bytes 262144 | tf_op jit(solution)/shard_map/pallas_call | solution.py:330
  171.5 0.1 collective-permute-start.1
  171.6 0.0 copy-done.5
  171.6 0.0 copy-start.6
  171.6 0.1 copy.37.momenta
  171.7 0.8 copy-done.6
  172.5 0.0 copy-start.4
  172.5 0.1 copy.38.noise
  172.5 3.4 %collective-permute-done.1.back = f32[4,16,3,128]{3,2,1,0:T(4,128)S(1)} collective-permute-done((f32[4,16,3,128]{3,2,1,0:T(4,128)S(1)}, f32[4,16,3,128]{3,2,1,0:T(4,128)S(1)}, u32[]{:S(2)}, u32[]{:S(2)}) %collective-permute-start.1) | collective-permute-done | bytes 98336 | tf_op jit(solution)/shard_map/ppermute | solution.py:501
  175.9 0.0 copy-done.4
  176.0 2.6 shard_map.160
  178.5 13.4 %all_to_all.15 = f32[8,48,128]{2,1,0:T(8,128)S(1)} all-to-all(f32[8,48,128]{2,1,0:T(8,128)S(1)} %get-tuple-element.11), channel_id=1, replica_groups=mesh['bead'=8,'space'=4] {'bead'}, dimensions={0} | all-to-all | bytes 393216 | tf_op jit(solution)/shard_map/all_to_all | solution.py:518
  191.9 3.4 %all-to-all-start = ((f32[8,72,128]{2,1,0:T(8,128)}), f32[8,72,128]{2,1,0:T(8,128)S(1)}, u32[]{:S(2)}, u32[]{:S(2)}) async-start(f32[8,72,128]{2,1,0:T(8,128)} %get-tuple-element.10), calls=%async_computation | async-start | bytes 589824 | tf_op jit(solution)/shard_map/all_to_all | solution.py:523
  195.4 0.1 collective-permute-start.2
  195.4 23.2 %shard_map.162.held = f32[1,16,8,128]{3,2,1,0:T(8,128)S(1)} custom-call(s32[42,2]{1,0:T(8,128)S(1)} %copy-done.2, f32[1,16,3,128]{3,2,1,0:T(4,128)S(1)} %reshape.61.position, f32[16,3,128]{2,1,0:T(4,128)S(1)} %get-tuple-element.26.params), custom_call_target="tpu_custom_call" | custom-call | flops 38010880 | bytes 262144 | tf_op jit(solution)/shard_map/pallas_call | solution.py:330
  218.7 0.0 collective-permute-done.2.next_position
  218.7 40.3 %shard_map.163 = (f32[1,16,3,128]{3,2,1,0:T(4,128)S(1)}, f32[1,16,3,128]{3,2,1,0:T(4,128)S(1)}) custom-call(s32[100,2]{1,0:T(8,128)S(1)} %copy-done, f32[1,16,3,128]{3,2,1,0:T(4,128)S(1)} %reshape.61.position, f32[16,3,128]{2,1,0:T(4,128)S(1)} %get-tuple-element.26.params, f32[1,16,3,128]{3,2,1,0:T(4,128)S(1)} %collective-permute-done.2.next_position, ...), custom_call_target="tpu_custom_call" | custom-call | flops 65536000 | bytes 262144 | tf_op jit(solution)/shard_map/pallas_call | solution.py:330
  259.0 0.5 collective-permute-start.3
  259.6 2.8 %collective-permute-done.3 = f32[1,16,3,128]{3,2,1,0:T(4,128)S(1)} collective-permute-done((f32[1,16,3,128]{3,2,1,0:T(4,128)S(1)}, f32[1,16,3,128]{3,2,1,0:T(4,128)S(1)}, u32[]{:S(2)}, u32[]{:S(2)}) %collective-permute-start.3) | collective-permute-done | bytes 24608 | tf_op jit(solution)/shard_map/ppermute | solution.py:525
  262.4 0.0 copy-start.1
  262.5 0.0 all-to-all-done.arrived
  262.5 0.7 copy-done.1
  263.2 0.4 shard_map.161
  263.6 16.9 %all_to_all.16 = f32[8,96,128]{2,1,0:T(8,128)S(1)} all-to-all(f32[8,96,128]{2,1,0:T(8,128)S(1)} %pad_maximum_fusion), channel_id=1, replica_groups=mesh['bead'=8,'space'=4] {'bead'}, dimensions={0} | all-to-all | bytes 786432 | tf_op jit(solution)/shard_map/all_to_all | solution.py:545
  280.5 0.0 copy-start.3
  280.6 0.7 copy-done.3
  281.2 1.0 shard_map.164
  282.2 0.6 copy.39
  282.9 0.6 copy.40
  (13 shorter events, 0.2 us)
Async XLA Ops:
  2.4 0.7 copy-start.7
  3.2 2.5 copy-start.2
  3.2 61.9 %collective-permute-start = (f32[5,16,3,128]{3,2,1,0:T(4,128)S(1)}, f32[5,16,3,128]{3,2,1,0:T(4,128)S(1)}, u32[]{:S(2)}, u32[]{:S(2)}) collective-permute-start(f32[5,16,3,128]{3,2,1,0:T(4,128)S(1)} %pad_maximum_fusion.1), channel_id=1, source_target_pairs={{1,0},{2,1},{3,2},{0,3},{5,4},{6,5},{7,6},{4,7},{9,8},{10,9},{11,1... | collective-permute-start | bytes 368648 | tf_op jit(solution)/shard_map/ppermute | solution.py:498
  65.2 0.8 copy-start
  66.0 105.6 %copy-start.5 = (f32[4,16,3,128]{3,1,2,0:T(8,128)S(1)}, f32[4,16,3,128]{3,1,2,0:T(8,128)}, u32[]{:S(2)}) copy-start(f32[4,16,3,128]{3,1,2,0:T(8,128)} %param.16) | copy-start | bytes 294916
  171.5 4.4 %collective-permute-start.1 = (f32[4,16,3,128]{3,2,1,0:T(4,128)S(1)}, f32[4,16,3,128]{3,2,1,0:T(4,128)S(1)}, u32[]{:S(2)}, u32[]{:S(2)}) collective-permute-start(f32[4,16,3,128]{3,2,1,0:T(4,128)S(1)} %get-tuple-element.9), channel_id=1, source_target_pairs={{0,1},{1,2},{2,3},{3,0},{4,5},{5,6},{6,7},{7,4},{8,9},{9,10},{10,1... | collective-permute-start | bytes 294920 | tf_op jit(solution)/shard_map/ppermute | solution.py:501
  171.6 0.9 copy-start.6
  172.5 3.5 %copy-start.4 = (f32[8,96]{1,0:T(8,128)S(1)}, f32[8,96]{1,0:T(8,128)}, u32[]{:S(2)}) copy-start(f32[8,96]{1,0:T(8,128)} %constant.22.clone.table) | copy-start | bytes 9220
  191.9 70.6 %all-to-all-start = ((f32[8,72,128]{2,1,0:T(8,128)}), f32[8,72,128]{2,1,0:T(8,128)S(1)}, u32[]{:S(2)}, u32[]{:S(2)}) async-start(f32[8,72,128]{2,1,0:T(8,128)} %get-tuple-element.10), calls=%async_computation | async-start | bytes 589824 | tf_op jit(solution)/shard_map/all_to_all | solution.py:523
  195.4 23.3 %collective-permute-start.2 = (f32[1,16,3,128]{3,2,1,0:T(4,128)S(1)}, f32[1,16,3,128]{3,2,1,0:T(4,128)S(1)}, u32[]{:S(2)}, u32[]{:S(2)}) collective-permute-start(f32[1,16,3,128]{3,2,1,0:T(4,128)S(1)} %reshape.61.position), channel_id=1, source_target_pairs={{1,0},{2,1},{3,2},{0,3},{5,4},{6,5},{7,6},{4,7},{9,8},{10,9},{11,1... | collective-permute-start | bytes 73736 | tf_op jit(solution)/shard_map/ppermute | solution.py:522
  259.0 3.4 %collective-permute-start.3 = (f32[1,16,3,128]{3,2,1,0:T(4,128)S(1)}, f32[1,16,3,128]{3,2,1,0:T(4,128)S(1)}, u32[]{:S(2)}, u32[]{:S(2)}) collective-permute-start(f32[1,16,3,128]{3,2,1,0:T(4,128)S(1)} %get-tuple-element.13), channel_id=1, source_target_pairs={{0,1},{1,2},{2,3},{3,0},{4,5},{5,6},{6,7},{7,4},{8,9},{9,10},{10,1... | collective-permute-start | bytes 73736 | tf_op jit(solution)/shard_map/ppermute | solution.py:525
  262.4 0.8 copy-start.1
  280.5 0.7 copy-start.3

commit v2 on v1

v2 whole, which is shorter than its diff:
```python
import functools

import jax
import jax.numpy as jnp
import numpy as np
from jax import lax
from jax.experimental import pallas as pl
from jax.experimental.pallas import tpu as pltpu
from jax.sharding import PartitionSpec as P

PC = 8
GY = 4
GZ = 4

TIME_STEP = 0.05
INVERSE_TEMP = 32.0
CENTROID_FRICTION = 1.0
INNER_CUT = 0.5
OUTER_CUT = 1.0
CUBE_ROOT_TWO = 2.0 ** (1.0 / 3.0)
F32 = jnp.float32
VMEM_LIMIT = 48 * 1024 * 1024


def mode_matrix(number):
    rows = np.arange(number, dtype=np.float64)[:, None]
    column = np.arange(number, dtype=np.float64)[None, :]
    phases = 2.0 * np.pi * rows * column / number
    factor = np.sqrt(2.0 / number)
    middle = np.cos(np.pi * rows) / np.sqrt(number)
    matrix = np.where(column < number / 2, factor * np.cos(phases), factor * np.sin(phases))
    matrix = np.where(column == number / 2, middle, matrix)
    return np.where(column == 0, 1.0 / np.sqrt(number), matrix)


def contract_matrix(full_count, reduced):
    selected = np.arange(reduced)
    selected = np.where(selected <= reduced // 2, selected, selected + full_count - reduced)
    chosen = mode_matrix(full_count)[:, selected]
    return np.sqrt(reduced / full_count) * (mode_matrix(reduced) @ chosen.T)


def step_matrices(number):
    index = np.arange(number, dtype=np.float64)
    frequency = 2.0 * (number / INVERSE_TEMP) * np.sin(np.pi * index / number)
    friction = np.where(index == 0, CENTROID_FRICTION, 2.0 * frequency)
    damping = np.exp(-friction * TIME_STEP)
    kicking = np.sqrt((1.0 - damping * damping) / INVERSE_TEMP)
    cosine = np.cos(frequency * TIME_STEP)
    sine = np.sin(frequency * TIME_STEP)
    drift = np.where(index == 0, TIME_STEP, sine / np.where(index == 0, 1.0, frequency))
    modes = mode_matrix(number)

    def over_beads(diagonal):
        return (modes * diagonal[None, :]) @ modes.T

    return np.array(
        [
            [over_beads(cosine), over_beads(drift * damping), over_beads(drift * kicking)],
            [
                over_beads(-frequency * sine),
                over_beads(cosine * damping),
                over_beads(cosine * kicking),
            ],
        ]
    )


def partner_lists(domain_cells):
    inside, across = [], []
    for one in range(domain_cells):
        near = []
        for two in range(domain_cells):
            step_y, step_z = two // GZ - one // GZ, two % GZ - one % GZ
            if abs(step_y) <= 1 and abs(step_z) <= 1:
                near.append((two, step_y, step_z))
        across.append(near)
        inside.append([entry for entry in near if entry[0] > one])
    return inside, across


def flat(lists):
    starts = np.cumsum([0] + [len(entries) for entries in lists]).astype(np.int32)
    return starts, np.array([value for entries in lists for entry in entries for value in entry], np.int32)


def pair_weight(h, radius_sq, terms, longer):
    inverse = pl.reciprocal(h, approx=True)
    if longer:
        quotient = terms[0] * inverse
        sixth = quotient * quotient * quotient
        outer = jnp.maximum(1.0 - radius_sq, 0.0)
        inner = jnp.maximum(1.0 - 4.0 * radius_sq, 0.0)
        switch = outer * outer - inner * inner
        slope = outer - 4.0 * inner
        return sixth * (
            (6.0 * sixth - 3.0) * (switch * inverse) + (2.0 * sixth - 2.0) * slope
        )
    quotient = terms[1] * inverse
    twice = quotient * quotient * quotient
    edge = jnp.maximum(terms[2] * inverse - 1.0, 2.0)
    bracket = edge * (twice - 1.0) - twice
    return (twice * bracket) * ((edge - 2.0) * h)


def weight_factor(longer):
    return 8.0 if longer else 64.0 / 3.0


def columns(block):
    few, lanes = block.shape
    return jnp.concatenate([block, jnp.zeros((8 - few, lanes), F32)], axis=0).T


def spread_rows(position, params, cell, beads, rows_ref, size_ref):
    lanes = position.shape[-1]
    sizes = columns(params[cell, 0:2, :])
    for kind in range(2):
        size_ref[kind] = jnp.broadcast_to(sizes[:, kind : kind + 1], (lanes, lanes))
    for bead in range(beads):
        block = columns(position[bead, cell])
        for axis in range(3):
            rows_ref[bead, axis] = jnp.broadcast_to(block[:, axis : axis + 1], (lanes, lanes))


def meet(
    longer, span, first, offset, partner, position, params, rows_ref, size_ref, total_ref, back_ref
):
    beads = position.shape[0]
    lanes = position.shape[-1]
    here = pl.ds(first, span)
    half = size_ref[0, here, :] + params[partner, 0:1, :]
    s2 = half * half
    terms = (s2,) if longer else (s2, CUBE_ROOT_TWO * s2, 0.75 + 3.0 * s2)
    depth = size_ref[1, here, :] * params[partner, 1:2, :]
    for bead in range(beads):
        place = position[bead, partner]
        apart = []
        for axis in range(3):
            other = place[axis : axis + 1, :] + offset[axis]
            apart.append(other - rows_ref[bead, axis, here, :])
        radius_sq = apart[0] * apart[0] + apart[1] * apart[1] + apart[2] * apart[2]
        weight = depth * pair_weight(radius_sq + s2, radius_sq, terms, longer)
        for axis in range(3):
            push = weight * apart[axis]
            total_ref[bead, partner, axis] += jnp.sum(push.reshape(span // 8, 8, lanes), axis=0)
            if back_ref is not None:
                back_ref[bead, axis, here, :] -= push


def fold_back(back_ref, bead):
    lanes = back_ref.shape[-1]
    column = lax.broadcasted_iota(jnp.int32, (lanes, 8), 1)
    sums = [jnp.sum(back_ref[bead, axis], axis=1, keepdims=True) for axis in range(3)]
    block = jnp.where(
        column == 0, sums[0], jnp.where(column == 1, sums[1], jnp.where(column == 2, sums[2], 0.0))
    )
    return block.T[0:3]


def fold_total(total_ref, bead, cell):
    return jnp.concatenate(
        [jnp.sum(total_ref[bead, cell, axis], axis=0, keepdims=True) for axis in range(3)], axis=0
    )


def pairs_kernel(
    longer, span, across, starts, partners, occupied, position, params, *rest
):
    if across:
        spread, spread_params, held, force_ref, other_ref = rest[:5]
    else:
        spread, spread_params, held = position, params, None
        force_ref = rest[0]
        other_ref = None
    total_ref, back_ref, rows_ref, size_ref = rest[-4:]
    beads, cells = position.shape[:2]
    total_ref[...] = jnp.zeros_like(total_ref)

    def per_cell(cell, carry):
        spread_rows(spread, spread_params, cell, beads, rows_ref, size_ref)
        back_ref[...] = jnp.zeros_like(back_ref)

        def per_span(index, carry):
            first = pl.multiple_of(index * span, span)
            common = (position, params, rows_ref, size_ref, total_ref)
            if not across:
                meet(longer, span, first, (0.0, 0.0, 0.0), cell, *common, None)

            def per_partner(entry, carry):
                offset = (
                    -1.0 if across else 0.0,
                    partners[3 * entry + 1].astype(F32),
                    partners[3 * entry + 2].astype(F32),
                )
                meet(longer, span, first, offset, partners[3 * entry], *common, back_ref)
                return carry

            return lax.fori_loop(starts[cell], starts[cell + 1], per_partner, carry)

        lax.fori_loop(0, lax.div(occupied[cell] + (span - 1), span), per_span, 0)
        for bead in range(beads):
            if across:
                other_ref[bead, cell] = weight_factor(longer) * fold_back(back_ref, bead)
            else:
                force_ref[bead, cell] = fold_back(back_ref, bead)
        return carry

    lax.fori_loop(0, cells, per_cell, 0)

    def finish(cell, carry):
        for bead in range(beads):
            total = fold_total(total_ref, bead, cell)
            if across:
                force_ref[bead, cell] = weight_factor(longer) * total + held[bead, cell]
            else:
                force_ref[bead, cell] = weight_factor(longer) * (total + force_ref[bead, cell])
        return carry

    lax.fori_loop(0, cells, finish, 0)


def call(kernel, inputs, smem, outputs, scratch, flops):
    return pl.pallas_call(
        kernel,
        out_shape=outputs,
        in_specs=[
            pl.BlockSpec(memory_space=pltpu.SMEM if place < smem else pltpu.VMEM)
            for place in range(len(inputs))
        ],
        scratch_shapes=scratch,
        compiler_params=pltpu.CompilerParams(vmem_limit_bytes=VMEM_LIMIT),
        cost_estimate=pl.CostEstimate(flops=flops, bytes_accessed=1 << 18, transcendentals=0),
    )(*inputs)


PAIR_FLOPS = 40 * 128 * 128


def pair_forces(position, params, occupied, next_position, next_params, next_occupied, longer):
    beads, cells, _, lanes = position.shape
    inside, across = partner_lists(cells)
    span = lanes // 2 if longer else lanes // 4
    scratch = [
        pltpu.VMEM((beads, cells, 3, 8, lanes), F32),
        pltpu.VMEM((beads, 3, lanes, lanes), F32),
        pltpu.VMEM((beads, 3, lanes, lanes), F32),
        pltpu.VMEM((2, lanes, lanes), F32),
    ]
    forces = jax.ShapeDtypeStruct((beads, cells, 3, lanes), F32)
    starts, entries = flat(inside)
    held = call(
        functools.partial(pairs_kernel, longer, span, False),
        (jnp.asarray(starts), jnp.asarray(entries), occupied, position, params),
        3,
        forces,
        scratch,
        PAIR_FLOPS * beads * (len(entries) // 3 + cells),
    )
    starts, entries = flat(across)
    return call(
        functools.partial(pairs_kernel, longer, span, True),
        (
            jnp.asarray(starts), jnp.asarray(entries), next_occupied, position, params,
            next_position, next_params, held,
        ),
        3,
        (forces, forces),
        scratch,
        PAIR_FLOPS * beads * (len(entries) // 3),
    )


def kick_kernel(
    piece_rows, groups, table, rank, position, momenta, noise, force, back, params, partial_ref, piece_ref
):
    beads, cells = position.shape[:2]
    holders = piece_ref.shape[0]
    reduced = table.shape[0]
    first = rank[0] * beads
    if holders * piece_rows > 3 * cells:
        piece_ref[...] = jnp.zeros_like(piece_ref)
    for cell in range(cells):
        mass = params[cell, 2:3, :]
        per_mass = 1.0 / mass
        per_root = lax.rsqrt(mass)
        per_root = per_root * (1.5 - 0.5 * mass * per_root * per_root)
        inputs = []
        for bead in range(beads):
            kicked = momenta[bead, cell] + 0.5 * TIME_STEP * (force[bead, cell] + back[bead, cell])
            inputs.append((position[bead, cell], kicked * per_mass, noise[bead, cell] * per_root))
        for bead in range(beads):
            for kind in range(3):
                base = (kind * beads + bead) * piece_rows
                if piece_rows % 3 == 0:
                    owner, row = divmod(3 * cell, piece_rows)
                    piece_ref[owner, base + row : base + row + 3, :] = inputs[bead][kind]
                else:
                    for axis in range(3):
                        owner, row = divmod(3 * cell + axis, piece_rows)
                        piece_ref[owner, base + row : base + row + 1, :] = inputs[bead][kind][
                            axis : axis + 1
                        ]
        for group in range(reduced):
            total = None
            for bead in range(beads):
                for kind in range(3):
                    term = table[group, kind * holders * beads + first + bead] * inputs[bead][kind]
                    total = term if total is None else total + term
            for copy in range(groups):
                partial_ref[group * groups + copy, 3 * cell : 3 * cell + 3, :] = total


def move_kernel(piece_rows, beads, matrix, arrived, out_ref, gathered):
    holders = arrived.shape[0]
    taken = 3 * beads
    given = 2 * beads
    for row in range(piece_rows):
        for holder in range(holders):
            gathered[row, holder * taken : (holder + 1) * taken, :] = arrived[
                holder, pl.ds(row, taken, stride=piece_rows), :
            ]
        moved = lax.dot_general(
            matrix[...],
            gathered[row],
            (((1,), (0,)), ((), ())),
            precision=lax.Precision.HIGHEST,
            preferred_element_type=F32,
        )
        for holder in range(holders):
            out_ref[holder, row * given : (row + 1) * given, :] = moved[
                holder * given : (holder + 1) * given
            ]


def finish_kernel(piece_rows, groups, table, rank, moved, slow, params, position_ref, momentum_ref):
    beads, cells = position_ref.shape[:2]
    given = 2 * beads
    reduced = table.shape[0]
    first = rank[0] * beads
    for cell in range(cells):
        mass = params[cell, 2:3, :]
        for bead in range(beads):
            def taken(kind):
                if piece_rows % 3 == 0:
                    owner, row = divmod(3 * cell, piece_rows)
                    return moved[owner, pl.ds(row * given + kind * beads + bead, 3, stride=given), :]
                rows = []
                for axis in range(3):
                    owner, row = divmod(3 * cell + axis, piece_rows)
                    place = row * given + kind * beads + bead
                    rows.append(moved[owner, place : place + 1, :])
                return jnp.concatenate(rows, axis=0)

            position_ref[bead, cell] = taken(0)
            total = mass * taken(1)
            for group in range(reduced):
                total = total + table[group, first + bead] * slow[
                    group * groups, 3 * cell : 3 * cell + 3, :
                ]
            momentum_ref[bead, cell] = total


def shards(positions, momenta, noise, atom_types, occupancy, type_sigma, type_eps, type_mass):
    beads, cells, _, lanes = positions.shape
    holders = lax.axis_size("bead")
    domains = lax.axis_size("space")
    rank = lax.axis_index("bead")
    total_beads = beads * holders
    rows = 3 * cells
    piece_rows = -(-rows // holders)
    held = max(1, PC // holders)
    groups = max(1, holders // PC)
    contract = contract_matrix(total_beads, PC)
    steps = step_matrices(total_beads)
    rank_table = rank.astype(jnp.int32).reshape(1)
    one_back = [((i + 1) % domains, i) for i in range(domains)]
    one_on = [(i, (i + 1) % domains) for i in range(domains)]

    codes = jnp.arange(type_sigma.shape[0])
    onehot = atom_types[..., None] == codes
    living = jnp.arange(lanes)[None, :] < occupancy[:, None]
    half_sigma = 0.5 * jnp.sum(jnp.where(onehot, type_sigma, 0.0), -1)
    root_eps = jnp.sqrt(jnp.sum(jnp.where(onehot, type_eps, 0.0), -1))
    mass = jnp.sum(jnp.where(onehot, type_mass, 0.0), -1)
    params = jnp.stack([half_sigma, jnp.where(living, root_eps, 0.0), mass], 1)

    stacked = jnp.concatenate([positions, params[None]], 0)
    next_stacked = lax.ppermute(stacked, "space", one_back)
    next_params = next_stacked[beads]
    next_occupied = jnp.sum((next_params[:, 1] > 0.0).astype(jnp.int32), -1)
    force, back = pair_forces(
        positions, params, occupancy, next_stacked[:beads], next_params, next_occupied, False
    )
    back = lax.ppermute(back, "space", one_on)

    position_map = np.concatenate([contract @ steps[0, kind] for kind in range(3)], axis=1)
    partial, pieces = call(
        functools.partial(kick_kernel, piece_rows, groups),
        (
            jnp.asarray(position_map, F32), rank_table, positions, momenta, noise, force, back,
            params,
        ),
        2,
        (
            jax.ShapeDtypeStruct((PC * groups, rows, lanes), F32),
            jax.ShapeDtypeStruct((holders, 3 * beads * piece_rows, lanes), F32),
        ),
        [],
        1 << 22,
    )
    arrived = lax.all_to_all(
        partial.reshape(holders, held * rows, lanes), "bead", split_axis=0, concat_axis=0, tiled=True
    )
    contracted = jnp.sum(arrived, 0).reshape(held, cells, 3, lanes)
    next_contracted = lax.ppermute(contracted, "space", one_back)
    pieces = lax.all_to_all(pieces, "bead", split_axis=0, concat_axis=0, tiled=True)
    slow, slow_back = pair_forces(
        contracted, params, occupancy, next_contracted, next_params, next_occupied, True
    )
    slow = slow + lax.ppermute(slow_back, "space", one_on)

    order = steps.reshape(2, 3, holders, beads, holders, beads).transpose(2, 0, 3, 4, 1, 5)
    order = order.reshape(2 * total_beads, 3 * total_beads)
    moved = call(
        functools.partial(move_kernel, piece_rows, beads),
        (jnp.asarray(order, F32), pieces),
        0,
        jax.ShapeDtypeStruct((holders, 2 * beads * piece_rows, lanes), F32),
        [pltpu.VMEM((piece_rows, 3 * total_beads, lanes), F32)],
        1 << 23,
    )
    moved_rows = 2 * beads * piece_rows
    sent = jnp.concatenate(
        [
            moved,
            jnp.broadcast_to(slow.reshape(1, held * rows, lanes), (holders, held * rows, lanes)),
        ],
        1,
    )
    got = lax.all_to_all(sent, "bead", split_axis=0, concat_axis=0, tiled=True)
    spread = 0.5 * TIME_STEP * (total_beads / PC) * contract
    shape = jax.ShapeDtypeStruct(positions.shape, F32)
    return call(
        functools.partial(finish_kernel, piece_rows, groups),
        (
            jnp.asarray(spread, F32), rank_table, got[:, :moved_rows],
            got[:, moved_rows:].reshape(holders * held, rows, lanes), params,
        ),
        2,
        (shape, shape),
        [],
        1 << 20,
    )


def solution(mesh):
    placed = (
        P("bead", "space", None, None),
        P("bead", "space", None, None),
        P("bead", "space", None, None),
        P("space", None),
        P("space"),
        P(),
        P(),
        P(),
    )
    return jax.shard_map(
        shards,
        mesh=mesh,
        in_specs=placed,
        out_specs=(P("bead", "space", None, None), P("bead", "space", None, None)),
        check_vma=False,
    )
```

time: 284 us -> 169 us (0.60)
  Pallas kernels: 232 us -> 119 us
    pallas_call x7, Pallas kernels: 232 us -> 119 us  [call(): pl.pallas_call(kernel, out_shape=outputs, in_specs=[pl.BlockSpec(memory_s...]
  transfers between devices with their start and end apart: 5 -> 5, of which waited for: 2 -> 2; matrix products, arithmetic and copies ran while one was open for 0% -> 0% of each run, Pallas kernels for 43% -> 39%
where the time goes in v2:
time: 169 us
  Pallas kernels  119 us (70%)
  blocking collectives  29.2 us (17%)
  waiting for transfers between devices  6.75 us (4%)
  starting transfers between devices  6.05 us (4%)
  local copies, waits for them, and re-layouts  5.99 us (4%)
    pallas_call x7, Pallas kernels, call(): pl.pallas_call(kernel, out_shape=outputs, in_specs=[pl.BlockSpec(memory_s...  119 us
    all_to_all x1, blocking collectives, shards(): got = lax.all_to_all(sent, 'bead', split_axis=0, concat_axis=0, tiled=True)  15.8 us
    all_to_all x1, blocking collectives, shards(): lax.all_to_all(partial.reshape(holders, held * rows, lanes), 'bead', spli...  13.4 us
    unnamed x23, local copies, waits for them, and re-layouts  4.58 us
    all_to_all x1, starting transfers between devices, shards(): lax.all_to_all(pieces, 'bead', split_axis=0, concat_axis=0, tiled=True)  3.42 us
    ppermute x1, waiting for transfers between devices, shards(): back = lax.ppermute(back, 'space', one_on)  3.41 us
  transfers between devices with their start and end apart: 5, of which 2 were waited for; matrix products, arithmetic and copies ran while one was open for 0% of the time, Pallas kernels for 39%

profile of v2, /device:TPU:0, one launch (start us, length us, event | category | flops | bytes accessed | tf_op | source)
XLA Modules:
  0.0 169.3 jit_solution(18208401513391380649)
XLA Ops:
  0.6 0.8 select_reduce_fusion.2
  1.4 0.9 copy.40.position
  2.4 0.0 copy-start.3
  2.4 0.6 copy-done.3
  3.1 0.1 compare_select_fusion
  3.2 0.0 copy-start.5
  3.2 0.0 copy-start.7
  3.3 2.5 %collective-permute-start = (f32[5,16,3,128]{3,2,1,0:T(4,128)S(1)}, f32[5,16,3,128]{3,2,1,0:T(4,128)S(1)}, u32[]{:S(2)}, u32[]{:S(2)}) collective-permute-start(f32[5,16,3,128]{3,2,1,0:T(4,128)S(1)} %pad_maximum_fusion.1), channel_id=1, source_target_pairs={{1,0},{2,1},{3,2},{0,3},{5,4},{6,5},{7,6},{4,7},{9,8},{10,9},{11,1... | collective-permute-start | bytes 368648 | tf_op jit(solution)/shard_map/ppermute | solution.py:389
  5.7 0.0 copy-done.5
  5.7 0.0 copy-done.7
  5.7 31.9 %shard_map.194.rest_2_ = f32[4,16,3,128]{3,2,1,0:T(4,128)S(1)} custom-call(s32[17]{0:T(128)S(1)} %copy-done.7, s32[126]{0:T(128)S(1)} %copy-done.5, s32[16]{0:T(128)S(1)} %copy-done.3, f32[4,16,3,128]{3,2,1,0:T(4,128)S(1)} %copy.40.position, f32[16,3,128]{2,1,0:T(4,128)S(1)} %get-tuple-element.25.params), custom_call_target="tpu_custom_call" | custom-call | flops 152043520 | bytes 262144 | tf_op jit(solution)/shard_map/pallas_call | solution.py:224
  37.7 0.0 collective-permute-done
  37.7 0.4 fusion.occupied
  38.1 0.0 copy-start.4
  38.1 0.0 copy-start.6
  38.1 0.6 copy-done.4
  38.8 0.0 copy-done.6
  38.8 0.0 copy-start.8
  38.8 49.2 %shard_map.195 = (f32[4,16,3,128]{3,2,1,0:T(4,128)S(1)}, f32[4,16,3,128]{3,2,1,0:T(4,128)S(1)}) custom-call(s32[17]{0:T(128)S(1)} %copy-done.6, s32[300]{0:T(512)S(1)} %copy-done.4, s32[16]{0:T(128)S(1)} %fusion.occupied, f32[4,16,3,128]{3,2,1,0:T(4,128)S(1)} %copy.40.position, f32[16,3,128]{2,1,0:T(4,128)S(1)} %get-tuple-element.25.params, ...), custom_call_target="tpu_custom_call" | custom-call | flops 262144000 | bytes 262144 | tf_op jit(solution)/shard_map/pallas_call | solution.py:224
  88.0 0.1 collective-permute-start.1
  88.0 0.0 copy-done.8
  88.0 0.0 copy-start.9
  88.0 0.1 copy.41.momenta
  88.1 0.8 copy-done.9
  88.9 0.0 copy-start.2
  88.9 0.1 copy.42.noise
  89.0 3.4 %collective-permute-done.1.back = f32[4,16,3,128]{3,2,1,0:T(4,128)S(1)} collective-permute-done((f32[4,16,3,128]{3,2,1,0:T(4,128)S(1)}, f32[4,16,3,128]{3,2,1,0:T(4,128)S(1)}, u32[]{:S(2)}, u32[]{:S(2)}) %collective-permute-start.1) | collective-permute-done | bytes 98336 | tf_op jit(solution)/shard_map/ppermute | solution.py:395
  92.4 0.0 copy-done.2
  92.4 2.6 %shard_map.196 = (f32[8,48,128]{2,1,0:T(8,128)S(1)}, f32[8,72,128]{2,1,0:T(8,128)}) custom-call(f32[8,96]{1,0:T(8,128)S(1)} %copy-done.2, s32[1]{0:T(128)} %bitcast.rank, f32[4,16,3,128]{3,2,1,0:T(4,128)S(1)} %copy.40.position, f32[4,16,3,128]{3,2,1,0:T(4,128)S(1)} %copy.41.momenta, f32[4,16,3,128]{3,2,1,0:T(4,128)S(1)} %copy.42.noise, ...), custom_call_target="tpu_custom_call" | custom-call | flops 4194304 | bytes 262144 | tf_op jit(solution)/shard_map/pallas_call | solution.py:224
  95.0 13.4 %all_to_all.15 = f32[8,48,128]{2,1,0:T(8,128)S(1)} all-to-all(f32[8,48,128]{2,1,0:T(8,128)S(1)} %get-tuple-element.11), channel_id=1, replica_groups=mesh['bead'=8,'space'=4] {'bead'}, dimensions={0} | all-to-all | bytes 393216 | tf_op jit(solution)/shard_map/all_to_all | solution.py:412
  108.3 3.4 %all-to-all-start = ((f32[8,72,128]{2,1,0:T(8,128)}), f32[8,72,128]{2,1,0:T(8,128)S(1)}, u32[]{:S(2)}, u32[]{:S(2)}) async-start(f32[8,72,128]{2,1,0:T(8,128)} %get-tuple-element.10), calls=%async_computation | async-start | bytes 589824 | tf_op jit(solution)/shard_map/all_to_all | solution.py:417
  111.8 0.1 collective-permute-start.2
  111.9 14.0 %shard_map.198.rest_2_ = f32[1,16,3,128]{3,2,1,0:T(4,128)S(1)} custom-call(s32[17]{0:T(128)S(1)} %copy-done.7, s32[126]{0:T(128)S(1)} %copy-done.5, s32[16]{0:T(128)S(1)} %copy-done.3, f32[1,16,3,128]{3,2,1,0:T(4,128)S(1)} %reshape.64.position, f32[16,3,128]{2,1,0:T(4,128)S(1)} %get-tuple-element.25.params), custom_call_target="tpu_custom_call" | custom-call | flops 38010880 | bytes 262144 | tf_op jit(solution)/shard_map/pallas_call | solution.py:224
  125.9 0.0 collective-permute-done.2.rest_0_
  125.9 20.0 %shard_map.199 = (f32[1,16,3,128]{3,2,1,0:T(4,128)S(1)}, f32[1,16,3,128]{3,2,1,0:T(4,128)S(1)}) custom-call(s32[17]{0:T(128)S(1)} %copy-done.6, s32[300]{0:T(512)S(1)} %copy-done.4, s32[16]{0:T(128)S(1)} %fusion.occupied, f32[1,16,3,128]{3,2,1,0:T(4,128)S(1)} %reshape.64.position, f32[16,3,128]{2,1,0:T(4,128)S(1)} %get-tuple-element.25.params, ...), custom_call_target="tpu_custom_call" | custom-call | flops 65536000 | bytes 262144 | tf_op jit(solution)/shard_map/pallas_call | solution.py:224
  145.9 0.1 collective-permute-start.3
  145.9 3.3 %collective-permute-done.3 = f32[1,16,3,128]{3,2,1,0:T(4,128)S(1)} collective-permute-done((f32[1,16,3,128]{3,2,1,0:T(4,128)S(1)}, f32[1,16,3,128]{3,2,1,0:T(4,128)S(1)}, u32[]{:S(2)}, u32[]{:S(2)}) %collective-permute-start.3) | collective-permute-done | bytes 24608 | tf_op jit(solution)/shard_map/ppermute | solution.py:421
  149.3 0.0 copy-start
  149.3 0.0 all-to-all-done.arrived
  149.3 0.7 copy-done
  150.0 0.4 shard_map.197
  150.5 15.8 %all_to_all.16 = f32[8,96,128]{2,1,0:T(8,128)S(1)} all-to-all(f32[8,96,128]{2,1,0:T(8,128)S(1)} %pad_maximum_fusion), channel_id=1, replica_groups=mesh['bead'=8,'space'=4] {'bead'}, dimensions={0} | all-to-all | bytes 786432 | tf_op jit(solution)/shard_map/all_to_all | solution.py:441
  166.3 0.0 copy-start.1
  166.3 0.7 copy-done.1
  167.0 1.0 shard_map.200
  168.0 0.6 copy.43
  168.6 0.6 copy.44
  (13 shorter events, 0.2 us)
Async XLA Ops:
  2.4 0.7 copy-start.3
  3.2 2.5 %copy-start.5 = (s32[126]{0:T(128)S(1)}, s32[126]{0:T(128)}, u32[]{:S(2)}) copy-start(s32[126]{0:T(128)} %constant.28.clone.partners) | copy-start | bytes 1516
  3.2 2.5 %copy-start.7 = (s32[17]{0:T(128)S(1)}, s32[17]{0:T(128)}, u32[]{:S(2)}) copy-start(s32[17]{0:T(128)} %constant.27.clone.starts) | copy-start | bytes 208
  3.3 34.4 %collective-permute-start = (f32[5,16,3,128]{3,2,1,0:T(4,128)S(1)}, f32[5,16,3,128]{3,2,1,0:T(4,128)S(1)}, u32[]{:S(2)}, u32[]{:S(2)}) collective-permute-start(f32[5,16,3,128]{3,2,1,0:T(4,128)S(1)} %pad_maximum_fusion.1), channel_id=1, source_target_pairs={{1,0},{2,1},{3,2},{0,3},{5,4},{6,5},{7,6},{4,7},{9,8},{10,9},{11,1... | collective-permute-start | bytes 368648 | tf_op jit(solution)/shard_map/ppermute | solution.py:389
  38.1 0.7 copy-start.4
  38.1 0.7 copy-start.6
  38.8 49.2 %copy-start.8 = (f32[4,16,3,128]{3,1,2,0:T(8,128)S(1)}, f32[4,16,3,128]{3,1,2,0:T(8,128)}, u32[]{:S(2)}) copy-start(f32[4,16,3,128]{3,1,2,0:T(8,128)} %param.20) | copy-start | bytes 294916
  88.0 4.4 %collective-permute-start.1 = (f32[4,16,3,128]{3,2,1,0:T(4,128)S(1)}, f32[4,16,3,128]{3,2,1,0:T(4,128)S(1)}, u32[]{:S(2)}, u32[]{:S(2)}) collective-permute-start(f32[4,16,3,128]{3,2,1,0:T(4,128)S(1)} %get-tuple-element.9), channel_id=1, source_target_pairs={{0,1},{1,2},{2,3},{3,0},{4,5},{5,6},{6,7},{7,4},{8,9},{9,10},{10,1... | collective-permute-start | bytes 294920 | tf_op jit(solution)/shard_map/ppermute | solution.py:395
  88.0 0.9 copy-start.9
  88.9 3.5 %copy-start.2 = (f32[8,96]{1,0:T(8,128)S(1)}, f32[8,96]{1,0:T(8,128)}, u32[]{:S(2)}) copy-start(f32[8,96]{1,0:T(8,128)} %constant.31.clone.table) | copy-start | bytes 9220
  108.3 41.0 %all-to-all-start = ((f32[8,72,128]{2,1,0:T(8,128)}), f32[8,72,128]{2,1,0:T(8,128)S(1)}, u32[]{:S(2)}, u32[]{:S(2)}) async-start(f32[8,72,128]{2,1,0:T(8,128)} %get-tuple-element.10), calls=%async_computation | async-start | bytes 589824 | tf_op jit(solution)/shard_map/all_to_all | solution.py:417
  111.8 14.0 %collective-permute-start.2 = (f32[1,16,3,128]{3,2,1,0:T(4,128)S(1)}, f32[1,16,3,128]{3,2,1,0:T(4,128)S(1)}, u32[]{:S(2)}, u32[]{:S(2)}) collective-permute-start(f32[1,16,3,128]{3,2,1,0:T(4,128)S(1)} %reshape.64.position), channel_id=1, source_target_pairs={{1,0},{2,1},{3,2},{0,3},{5,4},{6,5},{7,6},{4,7},{9,8},{10,9},{11,1... | collective-permute-start | bytes 73736 | tf_op jit(solution)/shard_map/ppermute | solution.py:416
  145.9 3.4 %collective-permute-start.3 = (f32[1,16,3,128]{3,2,1,0:T(4,128)S(1)}, f32[1,16,3,128]{3,2,1,0:T(4,128)S(1)}, u32[]{:S(2)}, u32[]{:S(2)}) collective-permute-start(f32[1,16,3,128]{3,2,1,0:T(4,128)S(1)} %get-tuple-element.13), channel_id=1, source_target_pairs={{0,1},{1,2},{2,3},{3,0},{4,5},{5,6},{6,7},{7,4},{8,9},{9,10},{10,1... | collective-permute-start | bytes 73736 | tf_op jit(solution)/shard_map/ppermute | solution.py:421
  149.3 0.8 copy-start
  166.3 0.7 copy-start.1

commit v3 on v2

--- a/solution.py
+++ b/solution.py
@@ -19,6 +19,7 @@
 OUTER_CUT = 1.0
 CUBE_ROOT_TWO = 2.0 ** (1.0 / 3.0)
 F32 = jnp.float32
+SPAN = 32
 VMEM_LIMIT = 48 * 1024 * 1024
 
 
@@ -67,19 +68,15 @@
 
 
 def partner_lists(domain_cells):
-    inside, across = [], []
+    lists = []
     for one in range(domain_cells):
         near = []
         for two in range(domain_cells):
             step_y, step_z = two // GZ - one // GZ, two % GZ - one % GZ
             if abs(step_y) <= 1 and abs(step_z) <= 1:
                 near.append((two, step_y, step_z))
-        across.append(near)
-        inside.append([entry for entry in near if entry[0] > one])
-    return inside, across
-
-
-def flat(lists):
+        later = [entry for entry in near if entry[0] > one]
+        lists.append(later + [(two + domain_cells, y, z) for two, y, z in near])
     starts = np.cumsum([0] + [len(entries) for entries in lists]).astype(np.int32)
     return starts, np.array([value for entries in lists for entry in entries for value in entry], np.int32)
 
@@ -112,112 +109,143 @@
     return jnp.concatenate([block, jnp.zeros((8 - few, lanes), F32)], axis=0).T
 
 
-def spread_rows(position, params, cell, beads, rows_ref, size_ref):
-    lanes = position.shape[-1]
+def spread_rows(position, params, cell, rows_ref, size_ref):
+    beads, lanes = position.shape[0], position.shape[-1]
     sizes = columns(params[cell, 0:2, :])
     for kind in range(2):
-        size_ref[kind] = jnp.broadcast_to(sizes[:, kind : kind + 1], (lanes, lanes))
+        size_ref[cell, kind] = jnp.broadcast_to(sizes[:, kind : kind + 1], (lanes, lanes))
     for bead in range(beads):
         block = columns(position[bead, cell])
         for axis in range(3):
-            rows_ref[bead, axis] = jnp.broadcast_to(block[:, axis : axis + 1], (lanes, lanes))
-
-
-def meet(
-    longer, span, first, offset, partner, position, params, rows_ref, size_ref, total_ref, back_ref
-):
-    beads = position.shape[0]
-    lanes = position.shape[-1]
-    here = pl.ds(first, span)
-    half = size_ref[0, here, :] + params[partner, 0:1, :]
-    s2 = half * half
-    terms = (s2,) if longer else (s2, CUBE_ROOT_TWO * s2, 0.75 + 3.0 * s2)
-    depth = size_ref[1, here, :] * params[partner, 1:2, :]
+            rows_ref[cell, bead, axis] = jnp.broadcast_to(
+                block[:, axis : axis + 1], (lanes, lanes)
+            )
+
+
+def meet(longer, cell, first, partners, refs):
+    lanes_ref, sizes_ref, rows_ref, size_ref, total_ref, back_ref = refs
+    beads, lanes = lanes_ref.shape[0], lanes_ref.shape[-1]
+    here = pl.ds(first, SPAN)
+    row_half, row_root = size_ref[cell, 0, here, :], size_ref[cell, 1, here, :]
+    known = []
+    for partner, _, _ in partners:
+        half = row_half + sizes_ref[partner, 0:1, :]
+        s2 = half * half
+        terms = (s2,) if longer else (s2, CUBE_ROOT_TWO * s2, 0.75 + 3.0 * s2)
+        known.append((s2, terms, row_root * sizes_ref[partner, 1:2, :]))
     for bead in range(beads):
-        place = position[bead, partner]
-        apart = []
+        rows = [rows_ref[cell, bead, axis, here, :] for axis in range(3)]
+        back = [None, None, None]
+        for (partner, step_y, step_z), (s2, terms, depth) in zip(partners, known):
+            place = lanes_ref[bead, partner]
+            apart = [
+                place[0:1] - rows[0], (place[1:2] + step_y) - rows[1], (place[2:3] + step_z) - rows[2]
+            ]
+            radius_sq = apart[0] * apart[0] + apart[1] * apart[1] + apart[2] * apart[2]
+            weight = depth * pair_weight(radius_sq + s2, radius_sq, terms, longer)
+            for axis in range(3):
+                push = weight * apart[axis]
+                back[axis] = push if back[axis] is None else back[axis] + push
+                if total_ref is not None:
+                    total_ref[partner, bead, axis] += jnp.sum(
+                        push.reshape(SPAN // 8, 8, lanes), axis=0
+                    )
         for axis in range(3):
-            other = place[axis : axis + 1, :] + offset[axis]
-            apart.append(other - rows_ref[bead, axis, here, :])
-        radius_sq = apart[0] * apart[0] + apart[1] * apart[1] + apart[2] * apart[2]
-        weight = depth * pair_weight(radius_sq + s2, radius_sq, terms, longer)
-        for axis in range(3):
-            push = weight * apart[axis]
-            total_ref[bead, partner, axis] += jnp.sum(push.reshape(span // 8, 8, lanes), axis=0)
-            if back_ref is not None:
-                back_ref[bead, axis, here, :] -= push
-
-
-def fold_back(back_ref, bead):
+            if total_ref is None:
+                back_ref[cell, bead, axis, here, :] = back[axis]
+            else:
+                back_ref[cell, bead, axis, here, :] += back[axis]
+
+
+def fold_back(back_ref, cell, bead):
     lanes = back_ref.shape[-1]
     column = lax.broadcasted_iota(jnp.int32, (lanes, 8), 1)
-    sums = [jnp.sum(back_ref[bead, axis], axis=1, keepdims=True) for axis in range(3)]
+    sums = [jnp.sum(back_ref[cell, bead, axis], axis=1, keepdims=True) for axis in range(3)]
     block = jnp.where(
         column == 0, sums[0], jnp.where(column == 1, sums[1], jnp.where(column == 2, sums[2], 0.0))
     )
     return block.T[0:3]
 
 
-def fold_total(total_ref, bead, cell):
+def fold_total(total_ref, cell, bead):
     return jnp.concatenate(
-        [jnp.sum(total_ref[bead, cell, axis], axis=0, keepdims=True) for axis in range(3)], axis=0
+        [jnp.sum(total_ref[cell, bead, axis], axis=0, keepdims=True) for axis in range(3)], axis=0
     )
 
 
 def pairs_kernel(
-    longer, span, across, starts, partners, occupied, position, params, *rest
+    longer, parts, starts, partners, occupied, position, params, next_position, next_params,
+    force_ref, other_ref, lanes_ref, sizes_ref, rows_ref, size_ref, total_ref, back_ref,
 ):
-    if across:
-        spread, spread_params, held, force_ref, other_ref = rest[:5]
-    else:
-        spread, spread_params, held = position, params, None
-        force_ref = rest[0]
-        other_ref = None
-    total_ref, back_ref, rows_ref, size_ref = rest[-4:]
-    beads, cells = position.shape[:2]
+    beads, cells, _, lanes = position.shape
+    factor = weight_factor(longer)
+    together = max(1, 4 // beads)
+    axis_row = lax.broadcasted_iota(jnp.int32, (3, lanes), 0)
+    layer = jnp.where(axis_row == 0, 1.0, 0.0)
+    for bead in range(beads):
+        lanes_ref[bead, 0:cells] = position[bead]
+        lanes_ref[bead, cells : 2 * cells] = next_position[bead] + layer[None]
+    sizes_ref[0:cells] = params[:, 0:2, :]
+    sizes_ref[cells : 2 * cells] = next_params[:, 0:2, :]
     total_ref[...] = jnp.zeros_like(total_ref)
 
+    def spread(index, carry):
+        for shift in range(together):
+            spread_rows(position, params, index * together + shift, rows_ref, size_ref)
+        return carry
+
+    lax.fori_loop(0, cells // together, spread, 0)
+    refs = (lanes_ref, sizes_ref, rows_ref, size_ref)
+
+    def entry_of(entry):
+        return (
+            partners[3 * entry],
+            partners[3 * entry + 1].astype(F32),
+            partners[3 * entry + 2].astype(F32),
+        )
+
     def per_cell(cell, carry):
-        spread_rows(spread, spread_params, cell, beads, rows_ref, size_ref)
-        back_ref[...] = jnp.zeros_like(back_ref)
+        begin, end = starts[cell], starts[cell + 1]
+        odd = lax.rem(end - begin, 2)
 
         def per_span(index, carry):
-            first = pl.multiple_of(index * span, span)
-            common = (position, params, rows_ref, size_ref, total_ref)
-            if not across:
-                meet(longer, span, first, (0.0, 0.0, 0.0), cell, *common, None)
-
-            def per_partner(entry, carry):
-                offset = (
-                    -1.0 if across else 0.0,
-                    partners[3 * entry + 1].astype(F32),
-                    partners[3 * entry + 2].astype(F32),
-                )
-                meet(longer, span, first, offset, partners[3 * entry], *common, back_ref)
+            firsts = [
+                pl.multiple_of((index * parts + part) * SPAN, SPAN) for part in range(parts)
+            ]
+            for first in firsts:
+                meet(longer, cell, first, [(cell, 0.0, 0.0)], refs + (None, back_ref))
+
+            def single(entry, carry):
+                for first in firsts:
+                    meet(longer, cell, first, [entry_of(entry)], refs + (total_ref, back_ref))
                 return carry
 
-            return lax.fori_loop(starts[cell], starts[cell + 1], per_partner, carry)
-
-        lax.fori_loop(0, lax.div(occupied[cell] + (span - 1), span), per_span, 0)
-        for bead in range(beads):
-            if across:
-                other_ref[bead, cell] = weight_factor(longer) * fold_back(back_ref, bead)
-            else:
-                force_ref[bead, cell] = fold_back(back_ref, bead)
+            def double(step, carry):
+                entry = begin + odd + 2 * step
+                both = [entry_of(entry), entry_of(entry + 1)]
+                for first in firsts:
+                    meet(longer, cell, first, both, refs + (total_ref, back_ref))
+                return carry
+
+            carry = lax.fori_loop(begin, begin + odd, single, carry)
+            return lax.fori_loop(0, lax.div(end - begin, 2), double, carry)
+
+        span = SPAN * parts
+        return lax.fori_loop(0, lax.div(occupied[cell] + (span - 1), span), per_span, carry)
+
+    lax.fori_loop(0, cells, per_cell, 0)
+
+    def finish(index, carry):
+        for shift in range(together):
+            cell = index * together + shift
+            alive = params[cell, 1:2, :] > 0.0
+            for bead in range(beads):
+                total = fold_total(total_ref, cell, bead) - fold_back(back_ref, cell, bead)
+                force_ref[bead, cell] = jnp.where(alive, factor * total, 0.0)
+                other_ref[bead, cell] = factor * fold_total(total_ref, cell + cells, bead)
         return carry
 
-    lax.fori_loop(0, cells, per_cell, 0)
-
-    def finish(cell, carry):
-        for bead in range(beads):
-            total = fold_total(total_ref, bead, cell)
-            if across:
-                force_ref[bead, cell] = weight_factor(longer) * total + held[bead, cell]
-            else:
-                force_ref[bead, cell] = weight_factor(longer) * (total + force_ref[bead, cell])
-        return carry
-
-    lax.fori_loop(0, cells, finish, 0)
+    lax.fori_loop(0, cells // together, finish, 0)
 
 
 def call(kernel, inputs, smem, outputs, scratch, flops):
@@ -237,37 +265,27 @@
 PAIR_FLOPS = 40 * 128 * 128
 
 
-def pair_forces(position, params, occupied, next_position, next_params, next_occupied, longer):
+def pair_forces(position, params, occupied, next_position, next_params, longer):
     beads, cells, _, lanes = position.shape
-    inside, across = partner_lists(cells)
-    span = lanes // 2 if longer else lanes // 4
-    scratch = [
-        pltpu.VMEM((beads, cells, 3, 8, lanes), F32),
-        pltpu.VMEM((beads, 3, lanes, lanes), F32),
-        pltpu.VMEM((beads, 3, lanes, lanes), F32),
-        pltpu.VMEM((2, lanes, lanes), F32),
-    ]
+    starts, entries = partner_lists(cells)
     forces = jax.ShapeDtypeStruct((beads, cells, 3, lanes), F32)
-    starts, entries = flat(inside)
-    held = call(
-        functools.partial(pairs_kernel, longer, span, False),
-        (jnp.asarray(starts), jnp.asarray(entries), occupied, position, params),
-        3,
-        forces,
-        scratch,
-        PAIR_FLOPS * beads * (len(entries) // 3 + cells),
-    )
-    starts, entries = flat(across)
     return call(
-        functools.partial(pairs_kernel, longer, span, True),
+        functools.partial(pairs_kernel, longer, lanes // SPAN if longer else 1),
         (
-            jnp.asarray(starts), jnp.asarray(entries), next_occupied, position, params,
-            next_position, next_params, held,
+            jnp.asarray(starts), jnp.asarray(entries), occupied, position, params, next_position,
+            next_params,
         ),
         3,
         (forces, forces),
-        scratch,
-        PAIR_FLOPS * beads * (len(entries) // 3),
+        [
+            pltpu.VMEM((beads, 2 * cells, 3, lanes), F32),
+            pltpu.VMEM((2 * cells, 2, lanes), F32),
+            pltpu.VMEM((cells, beads, 3, lanes, lanes), F32),
+            pltpu.VMEM((cells, 2, lanes, lanes), F32),
+            pltpu.VMEM((2 * cells, beads, 3, 8, lanes), F32),
+            pltpu.VMEM((cells, beads, 3, lanes, lanes), F32),
+        ],
+        PAIR_FLOPS * beads * (len(entries) // 3 + cells),
     )
 
 
@@ -388,9 +406,8 @@
     stacked = jnp.concatenate([positions, params[None]], 0)
     next_stacked = lax.ppermute(stacked, "space", one_back)
     next_params = next_stacked[beads]
-    next_occupied = jnp.sum((next_params[:, 1] > 0.0).astype(jnp.int32), -1)
     force, back = pair_forces(
-        positions, params, occupancy, next_stacked[:beads], next_params, next_occupied, False
+        positions, params, occupancy, next_stacked[:beads], next_params, False
     )
     back = lax.ppermute(back, "space", one_on)
 
@@ -416,7 +433,7 @@
     next_contracted = lax.ppermute(contracted, "space", one_back)
     pieces = lax.all_to_all(pieces, "bead", split_axis=0, concat_axis=0, tiled=True)
     slow, slow_back = pair_forces(
-        contracted, params, occupancy, next_contracted, next_params, next_occupied, True
+        contracted, params, occupancy, next_contracted, next_params, True
     )
     slow = slow + lax.ppermute(slow_back, "space", one_on)
 

time: 169 us -> 145 us (0.86)
  Pallas kernels: 119 us -> 86.5 us
  starting transfers between devices: 6.05 us -> 11.4 us
  blocking collectives: 29.2 us -> 32 us
    pallas_call x7 -> x5, Pallas kernels: 119 us -> 86.5 us  [call(): pl.pallas_call(kernel, out_shape=outputs, in_specs=[pl.BlockSpec(memory_s...]
    ppermute x1, starting transfers between devices: 0.06 us -> 3.01 us  [shards(): back = lax.ppermute(back, 'space', one_on)]
    ppermute x1, waiting for transfers between devices: 3.41 us -> 0.53 us  [shards(): back = lax.ppermute(back, 'space', one_on)]
    ppermute x1, waiting for transfers between devices: 0.01 us -> 2.84 us  [shards(): next_stacked = lax.ppermute(stacked, 'space', one_back)]
    ppermute x1, waiting for transfers between devices: 3.33 us -> 0.94 us  [shards(): slow = slow + lax.ppermute(slow_back, 'space', one_on)]
    ppermute x1, starting transfers between devices: 0.06 us -> 2.43 us  [shards(): slow = slow + lax.ppermute(slow_back, 'space', one_on)]
    all_to_all x1, blocking collectives: 15.8 us -> 18 us  [shards(): got = lax.all_to_all(sent, 'bead', split_axis=0, concat_axis=0, tiled=True)]
    unnamed x23 -> x19, local copies, waits for them, and re-layouts: 4.58 us -> 4.67 us
  transfers between devices with their start and end apart: 5 -> 5, of which waited for: 2 -> 4; matrix products, arithmetic and copies ran while one was open for 0% -> 0% of each run, Pallas kernels for 39% -> 15%
where the time goes in v3:
time: 145 us; the launch traced here: 144 us
  Pallas kernels  86.5 us (60%)
  blocking collectives  32 us (22%)
  starting transfers between devices  11.4 us (8%)
  local copies, waits for them, and re-layouts  6.08 us (4%)
  waiting for transfers between devices  5.91 us (4%)
    pallas_call x5, Pallas kernels, call(): pl.pallas_call(kernel, out_shape=outputs, in_specs=[pl.BlockSpec(memory_s...  86.5 us
    all_to_all x1, blocking collectives, shards(): got = lax.all_to_all(sent, 'bead', split_axis=0, concat_axis=0, tiled=True)  18 us
    all_to_all x1, blocking collectives, shards(): lax.all_to_all(partial.reshape(holders, held * rows, lanes), 'bead', spli...  14.1 us
    unnamed x19, local copies, waits for them, and re-layouts  4.67 us
    all_to_all x1, starting transfers between devices, shards(): lax.all_to_all(pieces, 'bead', split_axis=0, concat_axis=0, tiled=True)  3.42 us
    ppermute x1, starting transfers between devices, shards(): back = lax.ppermute(back, 'space', one_on)  3.01 us
  transfers between devices with their start and end apart: 5, of which 4 were waited for; matrix products, arithmetic and copies ran while one was open for 0% of the time, Pallas kernels for 15%

profile of v3, /device:TPU:0, one launch (start us, length us, event | category | flops | bytes accessed | tf_op | source)
XLA Modules:
  0.0 143.7 jit_solution(1627676643528772168)
XLA Ops:
  0.6 0.8 select_reduce_fusion.2
  1.4 0.9 copy.33.position
  2.4 0.0 copy-start.3
  2.4 0.6 copy-done.3
  3.1 0.1 compare_select_fusion
  3.2 2.5 %collective-permute-start = (f32[5,16,3,128]{3,2,1,0:T(4,128)S(1)}, f32[5,16,3,128]{3,2,1,0:T(4,128)S(1)}, u32[]{:S(2)}, u32[]{:S(2)}) collective-permute-start(f32[5,16,3,128]{3,2,1,0:T(4,128)S(1)} %pad_maximum_fusion.1), channel_id=1, source_target_pairs={{1,0},{2,1},{3,2},{0,3},{5,4},{6,5},{7,6},{4,7},{9,8},{10,9},{11,1... | collective-permute-start | bytes 368648 | tf_op jit(solution)/shard_map/ppermute | solution.py:407
  5.7 2.8 %collective-permute-done = f32[5,16,3,128]{3,2,1,0:T(4,128)S(1)} collective-permute-done((f32[5,16,3,128]{3,2,1,0:T(4,128)S(1)}, f32[5,16,3,128]{3,2,1,0:T(4,128)S(1)}, u32[]{:S(2)}, u32[]{:S(2)}) %collective-permute-start) | collective-permute-done | bytes 122912 | tf_op jit(solution)/shard_map/ppermute | solution.py:407
  8.5 0.0 copy-start.4
  8.6 0.0 copy-start.5
  8.6 0.6 copy-done.4
  9.2 0.0 copy-done.5
  9.2 0.0 copy-start.6
  9.2 61.3 %shard_map.158 = (f32[4,16,3,128]{3,2,1,0:T(4,128)S(1)}, f32[4,16,3,128]{3,2,1,0:T(4,128)S(1)}) custom-call(s32[17]{0:T(128)S(1)} %copy-done.5, s32[426]{0:T(512)S(1)} %copy-done.4, s32[16]{0:T(128)S(1)} %copy-done.3, f32[4,16,3,128]{3,2,1,0:T(4,128)S(1)} %copy.33.position, f32[16,3,128]{2,1,0:T(4,128)S(1)} %get-tuple-element.26.params, ...), custom_call_target="tpu_custom_call" | custom-call | flops 414187520 | bytes 262144 | tf_op jit(solution)/shard_map/pallas_call | solution.py:252
  70.5 3.0 %collective-permute-start.1 = (f32[4,16,3,128]{3,2,1,0:T(4,128)S(1)}, f32[4,16,3,128]{3,2,1,0:T(4,128)S(1)}, u32[]{:S(2)}, u32[]{:S(2)}) collective-permute-start(f32[4,16,3,128]{3,2,1,0:T(4,128)S(1)} %get-tuple-element.9), channel_id=1, source_target_pairs={{0,1},{1,2},{2,3},{3,0},{4,5},{5,6},{6,7},{7,4},{8,9},{9,10},{10,1... | collective-permute-start | bytes 294920 | tf_op jit(solution)/shard_map/ppermute | solution.py:412
  73.5 0.0 copy-done.6
  73.5 0.0 copy-start.7
  73.5 0.1 copy.34.momenta
  73.6 0.8 copy-done.7
  74.4 0.0 copy-start.2
  74.4 0.1 copy.35.noise
  74.5 0.5 collective-permute-done.1.back
  75.0 0.1 copy-done.2
  75.1 2.6 %shard_map.159 = (f32[8,48,128]{2,1,0:T(8,128)S(1)}, f32[8,72,128]{2,1,0:T(8,128)}) custom-call(f32[8,96]{1,0:T(8,128)S(1)} %copy-done.2, s32[1]{0:T(128)} %bitcast.rank, f32[4,16,3,128]{3,2,1,0:T(4,128)S(1)} %copy.33.position, f32[4,16,3,128]{3,2,1,0:T(4,128)S(1)} %copy.34.momenta, f32[4,16,3,128]{3,2,1,0:T(4,128)S(1)} %copy.35.noise, ...), custom_call_target="tpu_custom_call" | custom-call | flops 4194304 | bytes 262144 | tf_op jit(solution)/shard_map/pallas_call | solution.py:252
  77.7 14.1 %all_to_all.15 = f32[8,48,128]{2,1,0:T(8,128)S(1)} all-to-all(f32[8,48,128]{2,1,0:T(8,128)S(1)} %get-tuple-element.11), channel_id=1, replica_groups=mesh['bead'=8,'space'=4] {'bead'}, dimensions={0} | all-to-all | bytes 393216 | tf_op jit(solution)/shard_map/all_to_all | solution.py:429
  91.7 3.4 %all-to-all-start = ((f32[8,72,128]{2,1,0:T(8,128)}), f32[8,72,128]{2,1,0:T(8,128)S(1)}, u32[]{:S(2)}, u32[]{:S(2)}) async-start(f32[8,72,128]{2,1,0:T(8,128)} %get-tuple-element.10), calls=%async_computation | async-start | bytes 589824 | tf_op jit(solution)/shard_map/all_to_all | solution.py:434
  95.2 0.1 collective-permute-start.2
  95.3 1.6 %collective-permute-done.2.next_position = f32[1,16,3,128]{3,2,1,0:T(4,128)S(1)} collective-permute-done((f32[1,16,3,128]{3,2,1,0:T(4,128)S(1)}, f32[1,16,3,128]{3,2,1,0:T(4,128)S(1)}, u32[]{:S(2)}, u32[]{:S(2)}) %collective-permute-start.2) | collective-permute-done | bytes 24608 | tf_op jit(solution)/shard_map/ppermute | solution.py:433
  96.9 21.3 %shard_map.161 = (f32[1,16,3,128]{3,2,1,0:T(4,128)S(1)}, f32[1,16,3,128]{3,2,1,0:T(4,128)S(1)}) custom-call(s32[17]{0:T(128)S(1)} %copy-done.5, s32[426]{0:T(512)S(1)} %copy-done.4, s32[16]{0:T(128)S(1)} %copy-done.3, f32[1,16,3,128]{3,2,1,0:T(4,128)S(1)} %reshape.61.position, f32[16,3,128]{2,1,0:T(4,128)S(1)} %get-tuple-element.26.params, ...), custom_call_target="tpu_custom_call" | custom-call | flops 103546880 | bytes 262144 | tf_op jit(solution)/shard_map/pallas_call | solution.py:252
  118.2 2.4 %collective-permute-start.3 = (f32[1,16,3,128]{3,2,1,0:T(4,128)S(1)}, f32[1,16,3,128]{3,2,1,0:T(4,128)S(1)}, u32[]{:S(2)}, u32[]{:S(2)}) collective-permute-start(f32[1,16,3,128]{3,2,1,0:T(4,128)S(1)} %get-tuple-element.13), channel_id=1, source_target_pairs={{0,1},{1,2},{2,3},{3,0},{4,5},{5,6},{6,7},{7,4},{8,9},{9,10},{10,1... | collective-permute-start | bytes 73736 | tf_op jit(solution)/shard_map/ppermute | solution.py:438
  120.6 0.9 collective-permute-done.3
  121.6 0.0 copy-start
  121.6 0.0 all-to-all-done.arrived
  121.6 0.7 copy-done
  122.4 0.4 shard_map.160
  122.8 18.0 %all_to_all.16 = f32[8,96,128]{2,1,0:T(8,128)S(1)} all-to-all(f32[8,96,128]{2,1,0:T(8,128)S(1)} %pad_maximum_fusion), channel_id=1, replica_groups=mesh['bead'=8,'space'=4] {'bead'}, dimensions={0} | all-to-all | bytes 786432 | tf_op jit(solution)/shard_map/all_to_all | solution.py:458
  140.7 0.0 copy-start.1
  140.8 0.7 copy-done.1
  141.4 1.0 shard_map.162
  142.4 0.6 copy.36
  143.1 0.6 copy.37
  (13 shorter events, 0.2 us)
Async XLA Ops:
  2.4 0.7 copy-start.3
  3.2 5.3 %collective-permute-start = (f32[5,16,3,128]{3,2,1,0:T(4,128)S(1)}, f32[5,16,3,128]{3,2,1,0:T(4,128)S(1)}, u32[]{:S(2)}, u32[]{:S(2)}) collective-permute-start(f32[5,16,3,128]{3,2,1,0:T(4,128)S(1)} %pad_maximum_fusion.1), channel_id=1, source_target_pairs={{1,0},{2,1},{3,2},{0,3},{5,4},{6,5},{7,6},{4,7},{9,8},{10,9},{11,1... | collective-permute-start | bytes 368648 | tf_op jit(solution)/shard_map/ppermute | solution.py:407
  8.5 0.7 copy-start.4
  8.6 0.7 copy-start.5
  9.2 64.3 %copy-start.6 = (f32[4,16,3,128]{3,1,2,0:T(8,128)S(1)}, f32[4,16,3,128]{3,1,2,0:T(8,128)}, u32[]{:S(2)}) copy-start(f32[4,16,3,128]{3,1,2,0:T(8,128)} %param.16) | copy-start | bytes 294916
  70.5 4.5 %collective-permute-start.1 = (f32[4,16,3,128]{3,2,1,0:T(4,128)S(1)}, f32[4,16,3,128]{3,2,1,0:T(4,128)S(1)}, u32[]{:S(2)}, u32[]{:S(2)}) collective-permute-start(f32[4,16,3,128]{3,2,1,0:T(4,128)S(1)} %get-tuple-element.9), channel_id=1, source_target_pairs={{0,1},{1,2},{2,3},{3,0},{4,5},{5,6},{6,7},{7,4},{8,9},{9,10},{10,1... | collective-permute-start | bytes 294920 | tf_op jit(solution)/shard_map/ppermute | solution.py:412
  73.5 0.9 copy-start.7
  74.4 0.7 copy-start.2
  91.7 29.9 %all-to-all-start = ((f32[8,72,128]{2,1,0:T(8,128)}), f32[8,72,128]{2,1,0:T(8,128)S(1)}, u32[]{:S(2)}, u32[]{:S(2)}) async-start(f32[8,72,128]{2,1,0:T(8,128)} %get-tuple-element.10), calls=%async_computation | async-start | bytes 589824 | tf_op jit(solution)/shard_map/all_to_all | solution.py:434
  95.2 1.7 %collective-permute-start.2 = (f32[1,16,3,128]{3,2,1,0:T(4,128)S(1)}, f32[1,16,3,128]{3,2,1,0:T(4,128)S(1)}, u32[]{:S(2)}, u32[]{:S(2)}) collective-permute-start(f32[1,16,3,128]{3,2,1,0:T(4,128)S(1)} %reshape.61.position), channel_id=1, source_target_pairs={{1,0},{2,1},{3,2},{0,3},{5,4},{6,5},{7,6},{4,7},{9,8},{10,9},{11,1... | collective-permute-start | bytes 73736 | tf_op jit(solution)/shard_map/ppermute | solution.py:433
  118.2 3.4 %collective-permute-start.3 = (f32[1,16,3,128]{3,2,1,0:T(4,128)S(1)}, f32[1,16,3,128]{3,2,1,0:T(4,128)S(1)}, u32[]{:S(2)}, u32[]{:S(2)}) collective-permute-start(f32[1,16,3,128]{3,2,1,0:T(4,128)S(1)} %get-tuple-element.13), channel_id=1, source_target_pairs={{0,1},{1,2},{2,3},{3,0},{4,5},{5,6},{6,7},{7,4},{8,9},{9,10},{10,1... | collective-permute-start | bytes 73736 | tf_op jit(solution)/shard_map/ppermute | solution.py:438
  121.6 0.8 copy-start
  140.7 0.7 copy-start.1
